TPU v7x, 768 devices: a whole 4x8x12 slice. The times are simulated.
768 devices in a mesh: rep: 96 (over z, y), tp: 8 (over x, core).
Axes of the slice: x: 4, y: 8, z: 12, core: 2. Of those that a mesh axis runs over, the one named last changes fastest.
Arguments:
- momentum: float32 [96, 128, 28672], P('rep', None, 'tp')
- grad: bfloat16 [96, 128, 28672], P('rep', None, 'tp'), may hold values from -6 to 6
- weight: float32 [128, 28672], P(None, 'tp'), may hold values from -6 to 6
- indices: int32 [96, 2, 14336], P(None, None, 'tp'), may hold values from 0 to 4095, as said below
Outputs:
- moment_out: float32 [96, 128, 28672], P('rep', None, 'tp')
- weight_out: float32 [128, 28672], P(None, 'tp')
Inputs may be any that keep to these rules, and one draw needn't show every extreme that they name: `indices`: within each tile's 32 entries, the j-th lies in [j * 64 * 2, (j + 1) * 64 * 2), so they are distinct and rising.
All inputs are finite; a program needn't handle non-finite values.
Results may differ from a plain program's by a relative error of at most 0.0003.
Values sent between devices are 32-bit elements; how exact they have to be, the bound alone decides.
No kernel may reach another device: no remote copies, remote signals or barrier semaphores. Data moves between devices by JAX's collectives and lax.ppermute only.
A program may use at most 64 MiB of HBM per device.

v0:
```python
import jax
import jax.numpy as jnp
from jax import lax
from jax.sharding import PartitionSpec as P

TILE = 64
TOPK = 32


BETA = 0.999
RATE = 0.25
EPS = 1e-06


def dct_table():
    freq = jnp.arange(TILE, dtype=jnp.float32)[:, None]
    place = jnp.arange(TILE, dtype=jnp.float32)[None, :]
    table = jnp.cos(jnp.pi * (2.0 * place + 1.0) * freq / (2.0 * TILE))
    factor = jnp.where(freq == 0, jnp.sqrt(1.0 / TILE), jnp.sqrt(2.0 / TILE))
    return table * factor


def to_spectrum(field, table, paired):
    rows, cols = field.shape
    right = jnp.einsum(
        "rcn,kn->rck",
        field.reshape(rows, cols // 128, 128),
        paired,
        precision=lax.Precision.HIGHEST,
    )
    right = right.reshape(rows // TILE, TILE, cols)
    left = jnp.einsum("ij,ajf->aif", table, right, precision=lax.Precision.HIGHEST)
    left = left.reshape(rows // TILE, TILE, cols // TILE, TILE).transpose(0, 2, 1, 3)
    return left.reshape(rows // TILE, cols // TILE, TILE * TILE)


def from_spectrum(flat, table, paired):
    tile_rows, tile_cols, _ = flat.shape
    rows = tile_rows * TILE
    cols = tile_cols * TILE
    grid = (
        flat.reshape(tile_rows, tile_cols, TILE, TILE)
        .transpose(0, 2, 1, 3)
        .reshape(tile_rows, TILE, cols)
    )
    left = jnp.einsum("ij,aif->ajf", table, grid, precision=lax.Precision.HIGHEST)
    right = jnp.einsum(
        "rck,kn->rcn", left.reshape(rows, cols // 128, 128), paired, precision=lax.Precision.HIGHEST
    )
    return right.reshape(rows, cols)


def lane_offsets(chosen):
    band_width = TILE * TILE // TOPK
    band_start = jnp.arange(TOPK, dtype=jnp.int32) * band_width
    return chosen - band_start


def pick_values(coeffs, chosen):
    tile_rows, tile_cols, _ = coeffs.shape
    band_width = TILE * TILE // TOPK
    lane_blocks = coeffs.reshape(tile_rows, tile_cols, TOPK, band_width)
    offsets = lane_offsets(chosen)
    matches = offsets[..., None] == jnp.arange(band_width, dtype=jnp.int32)
    return jnp.sum(jnp.where(matches, lane_blocks, 0.0), axis=-1)


def spread_values(values, chosen):
    group_size, tile_rows, tile_cols, _ = values.shape
    band_width = TILE * TILE // TOPK
    offsets = lane_offsets(chosen)
    matches = offsets[..., None] == jnp.arange(band_width, dtype=jnp.int32)
    placed = jnp.sum(jnp.where(matches, values[..., None], 0.0), axis=0)
    return placed.reshape(tile_rows, tile_cols, TOPK * band_width)


def add_picked(summed, values, chosen):
    tile_rows, tile_cols, _ = summed.shape
    chosen = chosen.reshape(-1, tile_rows, tile_cols, TOPK)
    values = values.reshape(-1, tile_rows, tile_cols, TOPK)
    count = values.shape[0]
    group_size = 4 if count % 4 == 0 else 1
    if count == group_size:
        return spread_values(values, chosen)
    grouped_values = values.reshape(count // group_size, group_size, tile_rows, tile_cols, TOPK)
    grouped_chosen = chosen.reshape(count // group_size, group_size, tile_rows, tile_cols, TOPK)

    def accumulate(carry, item):
        group_values, group_chosen = item
        return (carry + spread_values(group_values, group_chosen), None)

    result, _ = lax.scan(accumulate, summed, (grouped_values, grouped_chosen))
    return result


def on_device(momentum, grad, weight, indices):
    table = dct_table()
    paired = jnp.kron(jnp.eye(2, dtype=jnp.float32), table)
    rows, cols = weight.shape
    tile_rows = rows // TILE
    tile_cols = cols // TILE
    decayed = BETA * momentum[0] + grad[0].astype(jnp.float32)
    coeffs = to_spectrum(decayed, table, paired)
    own_chosen = lax.dynamic_index_in_dim(indices, lax.axis_index("rep"), 0, keepdims=False)
    own_chosen = own_chosen.reshape(tile_rows, tile_cols, TOPK)
    picked = pick_values(coeffs, own_chosen)
    empty = jnp.zeros((tile_rows, tile_cols, TILE * TILE), jnp.float32)
    own_sparse = add_picked(empty, picked, own_chosen)
    moment_out = decayed - from_spectrum(own_sparse, table, paired)
    sent = picked.reshape(1, tile_rows, tile_cols * TOPK)
    every = lax.all_gather(sent, "rep", axis=0, tiled=True)
    summed = add_picked(empty, every, indices)
    decoded = from_spectrum(summed, table, paired)
    local_energy = jnp.sum(decoded * decoded)
    energy = lax.psum(local_energy, "tp")
    scale = jnp.sqrt(energy / (rows * cols * lax.axis_size("tp")) + EPS)
    weight_out = weight - RATE * decoded / scale
    return (moment_out[None], weight_out)


def solution(mesh):
    in_specs = (P("rep", None, "tp"), P("rep", None, "tp"), P(None, "tp"), P(None, None, "tp"))
    out_specs = (P("rep", None, "tp"), P(None, "tp"))
    return jax.shard_map(
        on_device, mesh=mesh, in_specs=in_specs, out_specs=out_specs, check_vma=False
    )
```

profile of v0, /device:TPU:1, one launch (start us, length us, event | category | flops | bytes accessed | tf_op | source)
XLA Modules:
  0.0 528.9 jit_solution(9658719056049365865)
XLA Ops:
  13.7 3.1 fusion.9
  21.9 4.6 convolution_bitcast_fusion.2
  26.4 3.6 reshape.183
  30.1 4.3 fusion
  35.4 4.0 reshape.196
  45.2 4.0 broadcast_in_dim.73
  52.1 4.0 eq.111
  56.1 5.5 %convolution_bitcast_fusion.1 = f32[2,64,3584]{2,1,0:T(8,128)} fusion(f32[2,64,3584]{2,1,0:T(8,128)} %broadcast_in_dim.73, s32[2,64,3584]{2,1,0:T(8,128)} %eq.111, s32[64,3584]{1,0:T(8,128)S(1)} %eq.118, f32[64]{0:T(128)S(1)} %get-tuple-element.68, f32[64]{0:T(128)S(1)} %get-tuple-element.69), kind=kOutput, calls=%fused_computation.7 | convolution fusion | flops 353251328 | bytes 6423040 | tf_op jit(solution)/shard_map/ij,aif->ajf/dot_general | solution.py:46
  64.4 4.4 fusion.3
  72.9 84.6 %all-gather.2.cloned.1.call-done = f32[96,2,1792]{2,1,0:T(2,128)} async-done(((f32[1,2,1792]{2,1,0:T(2,128)}), f32[96,2,1792]{2,1,0:T(2,128)}) %all-gather.2.cloned.1.call-update) | async-done | bytes 1376272 | tf_op jit(solution)/shard_map/all_gather | solution.py:111
  157.6 5.2 reshape.197
  162.7 308.5 %while.11 = (s32[]{:T(128)}, f32[2,56,4096]{2,1,0:T(8,128)}, s32[24,4,2,56,32]{4,3,2,1,0:T(8,128)}, f32[24,4,2,56,32]{4,3,2,1,0:T(8,128)}, s32[]{:T(128)}, /*index=5*/s32[]{:T(128)}) while((s32[]{:T(128)}, f32[2,56,4096]{2,1,0:T(8,128)}, s32[24,4,2,56,32]{4,3,2,1,0:T(8,128)}, f32[24,4,2,56,32]{4,3,2,1,0:T(8,128)}, s32[]{:T(128)}, ...), condition=%wide.region_4.5_spmd.clone, body=%wide.region_2.4_spmd.clone.sunk | while | flops 5978147 | bytes 11354463 | solution.py:92
  164.6 6.4 %select_reduce_fusion.2 = f32[2,56,32,128]{3,2,1,0:T(8,128)} fusion(f32[4,2,56,32]{3,2,1,0:T(8,128)S(1)} %dynamic-slice_bitcast_fusion.2, s32[4,2,56,32]{3,2,1,0:T(8,128)S(1)} %bitcast_subtract_fusion.3), kind=kLoop, calls=%fused_computation.clone.1 | loop fusion | flops 5046272 | bytes 1949696 | tf_op jit(solution)/shard_map/while/body/eval_jaxpr/reduce_sum | solution.py:73
  176.1 6.4 %select_reduce_fusion.2 = f32[2,56,32,128]{3,2,1,0:T(8,128)} fusion(f32[4,2,56,32]{3,2,1,0:T(8,128)S(1)} %dynamic-slice_bitcast_fusion.2, s32[4,2,56,32]{3,2,1,0:T(8,128)S(1)} %bitcast_subtract_fusion.3), kind=kLoop, calls=%fused_computation.clone.1 | loop fusion | flops 5046272 | bytes 1949696 | tf_op jit(solution)/shard_map/while/body/eval_jaxpr/reduce_sum | solution.py:73
  184.1 2.9 select_add_fusion.2
  189.0 6.4 %select_reduce_fusion.2 = f32[2,56,32,128]{3,2,1,0:T(8,128)} fusion(f32[4,2,56,32]{3,2,1,0:T(8,128)S(1)} %dynamic-slice_bitcast_fusion.2, s32[4,2,56,32]{3,2,1,0:T(8,128)S(1)} %bitcast_subtract_fusion.3), kind=kLoop, calls=%fused_computation.clone.1 | loop fusion | flops 5046272 | bytes 1949696 | tf_op jit(solution)/shard_map/while/body/eval_jaxpr/reduce_sum | solution.py:73
  197.0 2.9 select_add_fusion.2
  201.9 6.4 %select_reduce_fusion.2 = f32[2,56,32,128]{3,2,1,0:T(8,128)} fusion(f32[4,2,56,32]{3,2,1,0:T(8,128)S(1)} %dynamic-slice_bitcast_fusion.2, s32[4,2,56,32]{3,2,1,0:T(8,128)S(1)} %bitcast_subtract_fusion.3), kind=kLoop, calls=%fused_computation.clone.1 | loop fusion | flops 5046272 | bytes 1949696 | tf_op jit(solution)/shard_map/while/body/eval_jaxpr/reduce_sum | solution.py:73
  214.8 6.4 %select_reduce_fusion.2 = f32[2,56,32,128]{3,2,1,0:T(8,128)} fusion(f32[4,2,56,32]{3,2,1,0:T(8,128)S(1)} %dynamic-slice_bitcast_fusion.2, s32[4,2,56,32]{3,2,1,0:T(8,128)S(1)} %bitcast_subtract_fusion.3), kind=kLoop, calls=%fused_computation.clone.1 | loop fusion | flops 5046272 | bytes 1949696 | tf_op jit(solution)/shard_map/while/body/eval_jaxpr/reduce_sum | solution.py:73
  227.7 6.4 %select_reduce_fusion.2 = f32[2,56,32,128]{3,2,1,0:T(8,128)} fusion(f32[4,2,56,32]{3,2,1,0:T(8,128)S(1)} %dynamic-slice_bitcast_fusion.2, s32[4,2,56,32]{3,2,1,0:T(8,128)S(1)} %bitcast_subtract_fusion.3), kind=kLoop, calls=%fused_computation.clone.1 | loop fusion | flops 5046272 | bytes 1949696 | tf_op jit(solution)/shard_map/while/body/eval_jaxpr/reduce_sum | solution.py:73
  240.6 6.4 %select_reduce_fusion.2 = f32[2,56,32,128]{3,2,1,0:T(8,128)} fusion(f32[4,2,56,32]{3,2,1,0:T(8,128)S(1)} %dynamic-slice_bitcast_fusion.2, s32[4,2,56,32]{3,2,1,0:T(8,128)S(1)} %bitcast_subtract_fusion.3), kind=kLoop, calls=%fused_computation.clone.1 | loop fusion | flops 5046272 | bytes 1949696 | tf_op jit(solution)/shard_map/while/body/eval_jaxpr/reduce_sum | solution.py:73
  253.6 6.4 %select_reduce_fusion.2 = f32[2,56,32,128]{3,2,1,0:T(8,128)} fusion(f32[4,2,56,32]{3,2,1,0:T(8,128)S(1)} %dynamic-slice_bitcast_fusion.2, s32[4,2,56,32]{3,2,1,0:T(8,128)S(1)} %bitcast_subtract_fusion.3), kind=kLoop, calls=%fused_computation.clone.1 | loop fusion | flops 5046272 | bytes 1949696 | tf_op jit(solution)/shard_map/while/body/eval_jaxpr/reduce_sum | solution.py:73
  266.5 6.4 %select_reduce_fusion.2 = f32[2,56,32,128]{3,2,1,0:T(8,128)} fusion(f32[4,2,56,32]{3,2,1,0:T(8,128)S(1)} %dynamic-slice_bitcast_fusion.2, s32[4,2,56,32]{3,2,1,0:T(8,128)S(1)} %bitcast_subtract_fusion.3), kind=kLoop, calls=%fused_computation.clone.1 | loop fusion | flops 5046272 | bytes 1949696 | tf_op jit(solution)/shard_map/while/body/eval_jaxpr/reduce_sum | solution.py:73
  274.5 2.9 select_add_fusion.2
  279.4 6.4 %select_reduce_fusion.2 = f32[2,56,32,128]{3,2,1,0:T(8,128)} fusion(f32[4,2,56,32]{3,2,1,0:T(8,128)S(1)} %dynamic-slice_bitcast_fusion.2, s32[4,2,56,32]{3,2,1,0:T(8,128)S(1)} %bitcast_subtract_fusion.3), kind=kLoop, calls=%fused_computation.clone.1 | loop fusion | flops 5046272 | bytes 1949696 | tf_op jit(solution)/shard_map/while/body/eval_jaxpr/reduce_sum | solution.py:73
  292.3 6.4 %select_reduce_fusion.2 = f32[2,56,32,128]{3,2,1,0:T(8,128)} fusion(f32[4,2,56,32]{3,2,1,0:T(8,128)S(1)} %dynamic-slice_bitcast_fusion.2, s32[4,2,56,32]{3,2,1,0:T(8,128)S(1)} %bitcast_subtract_fusion.3), kind=kLoop, calls=%fused_computation.clone.1 | loop fusion | flops 5046272 | bytes 1949696 | tf_op jit(solution)/shard_map/while/body/eval_jaxpr/reduce_sum | solution.py:73
  305.2 6.4 %select_reduce_fusion.2 = f32[2,56,32,128]{3,2,1,0:T(8,128)} fusion(f32[4,2,56,32]{3,2,1,0:T(8,128)S(1)} %dynamic-slice_bitcast_fusion.2, s32[4,2,56,32]{3,2,1,0:T(8,128)S(1)} %bitcast_subtract_fusion.3), kind=kLoop, calls=%fused_computation.clone.1 | loop fusion | flops 5046272 | bytes 1949696 | tf_op jit(solution)/shard_map/while/body/eval_jaxpr/reduce_sum | solution.py:73
  318.1 6.4 %select_reduce_fusion.2 = f32[2,56,32,128]{3,2,1,0:T(8,128)} fusion(f32[4,2,56,32]{3,2,1,0:T(8,128)S(1)} %dynamic-slice_bitcast_fusion.2, s32[4,2,56,32]{3,2,1,0:T(8,128)S(1)} %bitcast_subtract_fusion.3), kind=kLoop, calls=%fused_computation.clone.1 | loop fusion | flops 5046272 | bytes 1949696 | tf_op jit(solution)/shard_map/while/body/eval_jaxpr/reduce_sum | solution.py:73
  331.0 6.4 %select_reduce_fusion.2 = f32[2,56,32,128]{3,2,1,0:T(8,128)} fusion(f32[4,2,56,32]{3,2,1,0:T(8,128)S(1)} %dynamic-slice_bitcast_fusion.2, s32[4,2,56,32]{3,2,1,0:T(8,128)S(1)} %bitcast_subtract_fusion.3), kind=kLoop, calls=%fused_computation.clone.1 | loop fusion | flops 5046272 | bytes 1949696 | tf_op jit(solution)/shard_map/while/body/eval_jaxpr/reduce_sum | solution.py:73
  344.0 6.4 %select_reduce_fusion.2 = f32[2,56,32,128]{3,2,1,0:T(8,128)} fusion(f32[4,2,56,32]{3,2,1,0:T(8,128)S(1)} %dynamic-slice_bitcast_fusion.2, s32[4,2,56,32]{3,2,1,0:T(8,128)S(1)} %bitcast_subtract_fusion.3), kind=kLoop, calls=%fused_computation.clone.1 | loop fusion | flops 5046272 | bytes 1949696 | tf_op jit(solution)/shard_map/while/body/eval_jaxpr/reduce_sum | solution.py:73
  352.0 2.9 select_add_fusion.2
  356.9 6.4 %select_reduce_fusion.2 = f32[2,56,32,128]{3,2,1,0:T(8,128)} fusion(f32[4,2,56,32]{3,2,1,0:T(8,128)S(1)} %dynamic-slice_bitcast_fusion.2, s32[4,2,56,32]{3,2,1,0:T(8,128)S(1)} %bitcast_subtract_fusion.3), kind=kLoop, calls=%fused_computation.clone.1 | loop fusion | flops 5046272 | bytes 1949696 | tf_op jit(solution)/shard_map/while/body/eval_jaxpr/reduce_sum | solution.py:73
  369.8 6.4 %select_reduce_fusion.2 = f32[2,56,32,128]{3,2,1,0:T(8,128)} fusion(f32[4,2,56,32]{3,2,1,0:T(8,128)S(1)} %dynamic-slice_bitcast_fusion.2, s32[4,2,56,32]{3,2,1,0:T(8,128)S(1)} %bitcast_subtract_fusion.3), kind=kLoop, calls=%fused_computation.clone.1 | loop fusion | flops 5046272 | bytes 1949696 | tf_op jit(solution)/shard_map/while/body/eval_jaxpr/reduce_sum | solution.py:73
  382.7 6.4 %select_reduce_fusion.2 = f32[2,56,32,128]{3,2,1,0:T(8,128)} fusion(f32[4,2,56,32]{3,2,1,0:T(8,128)S(1)} %dynamic-slice_bitcast_fusion.2, s32[4,2,56,32]{3,2,1,0:T(8,128)S(1)} %bitcast_subtract_fusion.3), kind=kLoop, calls=%fused_computation.clone.1 | loop fusion | flops 5046272 | bytes 1949696 | tf_op jit(solution)/shard_map/while/body/eval_jaxpr/reduce_sum | solution.py:73
  395.6 6.4 %select_reduce_fusion.2 = f32[2,56,32,128]{3,2,1,0:T(8,128)} fusion(f32[4,2,56,32]{3,2,1,0:T(8,128)S(1)} %dynamic-slice_bitcast_fusion.2, s32[4,2,56,32]{3,2,1,0:T(8,128)S(1)} %bitcast_subtract_fusion.3), kind=kLoop, calls=%fused_computation.clone.1 | loop fusion | flops 5046272 | bytes 1949696 | tf_op jit(solution)/shard_map/while/body/eval_jaxpr/reduce_sum | solution.py:73
  408.5 6.4 %select_reduce_fusion.2 = f32[2,56,32,128]{3,2,1,0:T(8,128)} fusion(f32[4,2,56,32]{3,2,1,0:T(8,128)S(1)} %dynamic-slice_bitcast_fusion.2, s32[4,2,56,32]{3,2,1,0:T(8,128)S(1)} %bitcast_subtract_fusion.3), kind=kLoop, calls=%fused_computation.clone.1 | loop fusion | flops 5046272 | bytes 1949696 | tf_op jit(solution)/shard_map/while/body/eval_jaxpr/reduce_sum | solution.py:73
  421.5 6.4 %select_reduce_fusion.2 = f32[2,56,32,128]{3,2,1,0:T(8,128)} fusion(f32[4,2,56,32]{3,2,1,0:T(8,128)S(1)} %dynamic-slice_bitcast_fusion.2, s32[4,2,56,32]{3,2,1,0:T(8,128)S(1)} %bitcast_subtract_fusion.3), kind=kLoop, calls=%fused_computation.clone.1 | loop fusion | flops 5046272 | bytes 1949696 | tf_op jit(solution)/shard_map/while/body/eval_jaxpr/reduce_sum | solution.py:73
  429.5 2.9 select_add_fusion.2
  434.4 6.4 %select_reduce_fusion.2 = f32[2,56,32,128]{3,2,1,0:T(8,128)} fusion(f32[4,2,56,32]{3,2,1,0:T(8,128)S(1)} %dynamic-slice_bitcast_fusion.2, s32[4,2,56,32]{3,2,1,0:T(8,128)S(1)} %bitcast_subtract_fusion.3), kind=kLoop, calls=%fused_computation.clone.1 | loop fusion | flops 5046272 | bytes 1949696 | tf_op jit(solution)/shard_map/while/body/eval_jaxpr/reduce_sum | solution.py:73
  447.3 6.4 %select_reduce_fusion.2 = f32[2,56,32,128]{3,2,1,0:T(8,128)} fusion(f32[4,2,56,32]{3,2,1,0:T(8,128)S(1)} %dynamic-slice_bitcast_fusion.2, s32[4,2,56,32]{3,2,1,0:T(8,128)S(1)} %bitcast_subtract_fusion.3), kind=kLoop, calls=%fused_computation.clone.1 | loop fusion | flops 5046272 | bytes 1949696 | tf_op jit(solution)/shard_map/while/body/eval_jaxpr/reduce_sum | solution.py:73
  460.2 6.4 %select_reduce_fusion.2 = f32[2,56,32,128]{3,2,1,0:T(8,128)} fusion(f32[4,2,56,32]{3,2,1,0:T(8,128)S(1)} %dynamic-slice_bitcast_fusion.2, s32[4,2,56,32]{3,2,1,0:T(8,128)S(1)} %bitcast_subtract_fusion.3), kind=kLoop, calls=%fused_computation.clone.1 | loop fusion | flops 5046272 | bytes 1949696 | tf_op jit(solution)/shard_map/while/body/eval_jaxpr/reduce_sum | solution.py:73
  471.2 3.9 reshape.187
  475.1 6.0 %copy.62 = f32[2,64,56,64]{3,2,1,0:T(8,128)} copy(f32[2,64,56,64]{3,1,2,0:T(8,128)} %bitcast.60) | data formatting | bytes 3670016 | tf_op jit(solution)/shard_map/transpose | solution.py:43
  481.1 3.2 reshape.188
  484.4 3.2 convolution_bitcast_fusion
  489.2 4.8 multiply_reduce_fusion
  494.0 20.6 %psum.7 = f32[]{:T(128)} all-reduce(f32[]{:T(128)} %get-tuple-element.66), channel_id=1, replica_groups=mesh['rep'=96,'tp'=8] {'tp'}, use_global_device_ids=true, to_apply=%region_6.7 | all-reduce | flops 1 | bytes 8 | tf_op jit(solution)/shard_map/psum | solution.py:115
  518.6 3.5 sub.44
  (155 shorter events, 172.3 us)
Async XLA Ops:
  7.2 3.1 copy-start
  7.2 150.4 %all-gather.2.cloned.1.call-start = ((), (), s32[]{:S(2)}) async-start(), calls=%async_computation | async-start | bytes 1390592 | tf_op jit(solution)/shard_map/all_gather | solution.py:111
  30.1 5.3 %copy-start.1 = (s32[96,2,1792]{2,1,0:T(2,128)S(1)}, s32[96,2,1792]{2,1,0:T(2,128)}, u32[]{:S(2)}) copy-start(s32[96,2,1792]{2,1,0:T(2,128)} %param.9) | copy-start | bytes 4128772
Sparse Core Ops, SparseCore 0:
  35.4 122.0 all-gather.1
where the time goes:
time: 532 us; the launch traced here: 529 us
  other arithmetic  259 us (49%)
  local copies, waits for them, and re-layouts  124 us (23%)
  waiting for transfers between devices  84.6 us (16%)
  matrix products  25.5 us (5%)
  blocking collectives  20.6 us (4%)
  between operations  14.8 us (3%)
    reduce_sum x24, other arithmetic, spread_values(): placed = jnp.sum(jnp.where(matches, values[..., None], 0.0), axis=0)  154 us
    all_gather x1, waiting for transfers between devices, on_device(): every = lax.all_gather(sent, 'rep', axis=0, tiled=True)  84.6 us
    add x24, other arithmetic, accumulate(): return (carry + spread_values(group_values, group_chosen), None)  69.2 us
    reshape x24, local copies, waits for them, and re-layouts, spread_values(): return placed.reshape(tile_rows, tile_cols, TOPK * band_width)  38.6 us
    broadcast_in_dim x27, local copies, waits for them, and re-layouts, spread_values(): placed = jnp.sum(jnp.where(matches, values[..., None], 0.0), axis=0)  29.5 us
    sub x25, other arithmetic, lane_offsets(): return chosen - band_start  22.9 us
    psum x1, blocking collectives, on_device(): energy = lax.psum(local_energy, 'tp')  20.6 us
  transfers between devices with their start and end apart: 1, of which 1 were waited for; matrix products, arithmetic and copies ran while one was open for 7% of the time, Pallas kernels for 0%

commit v1 on v0

v1 whole, which is shorter than its diff:
```python
import jax
import jax.numpy as jnp
import ml_dtypes
import numpy as np
from jax import lax
from jax.experimental import pallas as pl
from jax.experimental.pallas import tpu as pltpu
from jax.sharding import PartitionSpec as P

TILE = 64
TOPK = 32
BAND = TILE * TILE // TOPK
BETA = 0.999
RATE = 0.25
EPS = 1e-06

ROWS = 128
COLS = 3584
N_REP = 96
N_TP = 8
LANES = 128
GROUPS = 14
PAIRS = 2 * GROUPS
NONE = 127
VMEM = 60 << 20
HALVES = 2

Z, Y = 12, 8
ZR, YR = 3, 2
ZQ, YQ = Z // ZR, Y // YR


def far_groups():
    return [
        [(zq * ZR + zr) * Y + yq * YR + yr for zq in range(ZQ) for yq in range(YQ)]
        for zr in range(ZR)
        for yr in range(YR)
    ]


def near_groups():
    return [
        [(zq * ZR + zr) * Y + yq * YR + yr for zr in range(ZR) for yr in range(YR)]
        for zq in range(ZQ)
        for yq in range(YQ)
    ]


def replica_at():
    return [r for group in far_groups() for r in group]


def dct():
    k = np.arange(TILE, dtype=np.float64)[:, None]
    n = np.arange(TILE, dtype=np.float64)[None, :]
    c = np.where(k == 0, np.sqrt(1.0 / TILE), np.sqrt(2.0 / TILE))
    return c * np.cos(np.pi * (2 * n + 1) * k / (2 * TILE))


def two(x):
    x = np.asarray(x, np.float32)
    hi = x.astype(ml_dtypes.bfloat16)
    lo = (x - hi.astype(np.float32)).astype(ml_dtypes.bfloat16)
    return np.stack([hi, lo])


def split(x):
    hi = x.astype(jnp.bfloat16)
    return hi, (x - hi.astype(jnp.float32)).astype(jnp.bfloat16)


def mm(a, b):
    return jnp.dot(a, b, preferred_element_type=jnp.float32)


def times(x, table):
    hi, lo = split(x)
    return mm(hi, table[0]) + (mm(lo, table[0]) + mm(hi, table[1]))


def times_left(table, x):
    hi, lo = split(x)
    return mm(table[0], hi) + (mm(table[0], lo) + mm(table[1], hi))


def iota(shape, dim):
    return lax.broadcasted_iota(jnp.int32, shape, dim)


def stack(ref, n, width, axis=0):
    return jnp.concatenate([ref[:, width * g : width * g + width] for g in range(n)], axis=axis)


def kept_coefficients(momentum, grad, chosen, left, right, spread, wide):
    n = momentum.shape[2] // 256
    for g in range(n):
        c = slice(256 * g, 256 * g + 256)
        decayed = BETA * momentum[0, :, c] + grad[0, :, c].astype(jnp.float32)
        wide[ROWS * g : ROWS * g + ROWS, :] = decayed
    first = times(wide[...], right)
    row = iota((ROWS, LANES), 0)
    lane = iota((ROWS, LANES), 1)
    own = (row % TILE) // 2 == lane % TOPK
    base = (lane[:1] % TOPK) * BAND
    offsets = []
    for g in range(n):
        offset = chosen[0, :, LANES * g : LANES * g + LANES] - base
        per_row = jnp.where(row < TILE, offset[0:1], offset[1:2])
        offsets.append(jnp.where(own, per_row, 0).astype(jnp.float32).astype(jnp.bfloat16))
    offsets = mm(jnp.concatenate(offsets, axis=0), spread[...])
    row = iota((ROWS, 256), 0)
    lane = iota((ROWS, 256), 1)
    place = ((row % 2) * TILE + lane % TILE).astype(jnp.float32)
    for g in range(n):
        at = slice(ROWS * g, ROWS * g + ROWS)
        coeffs = times_left(left, first[at])
        wide[at, :] = jnp.where(offsets[at] == place, coeffs, 0.0)
    return own


def pick_kernel(rep, momentum, grad, chosen, left, right, spread, gather, out, wide):
    del rep
    own = kept_coefficients(momentum, grad, chosen, left, right, spread, wide)
    hi, lo = split(wide[...])
    both = mm(hi, gather[...]) + mm(lo, gather[...])
    for g in range(momentum.shape[2] // 256):
        block = jnp.where(own, both[ROWS * g : ROWS * g + ROWS], 0.0)
        top = jnp.sum(block[:TILE], axis=0, keepdims=True)
        low = jnp.sum(block[TILE:], axis=0, keepdims=True)
        value = jnp.concatenate([top, low], axis=0)
        for k in range(out.shape[0]):
            out[k, :, LANES * g : LANES * g + LANES] = value


def residual_kernel(rep, momentum, grad, chosen, left, right, spread, left_back, right_back, out, wide):
    del rep
    kept_coefficients(momentum, grad, chosen, left, right, spread, wide)
    n = momentum.shape[2] // 256
    for g in range(n):
        at = slice(ROWS * g, ROWS * g + ROWS)
        wide[at, :] = times_left(left_back, wide[at, :])
    back = times(wide[...], right_back)
    for g in range(n):
        c = slice(256 * g, 256 * g + 256)
        decayed = BETA * momentum[0, :, c] + grad[0, :, c].astype(jnp.float32)
        out[0, :, c] = decayed - back[ROWS * g : ROWS * g + ROWS]


def table_kernel(chosen, out, deep, rows):
    half = jnp.bfloat16
    order = replica_at()

    def one(step, carry):
        at = pl.multiple_of(step * LANES, LANES)
        base = (iota((N_REP, LANES), 1) % TOPK) * BAND
        rows[...] = (chosen[:, pl.ds(at, LANES)] - base).astype(jnp.float32)
        place = [(iota((16, LANES), 0) + 16 * v).astype(jnp.float32).astype(half) for v in range(BAND // 16)]
        none = jnp.full((16, LANES), NONE, half)
        first = [none] * (BAND // 16)
        after = [none] * (N_REP // 16)
        blocks = []
        for v in range(0, N_REP, 16):
            parts = [rows[pl.ds(order[v + q], YQ, stride=YR), :] for q in range(0, 16, YQ)]
            blocks.append(jnp.concatenate(parts, axis=0).astype(half))
        for p in reversed(range(N_REP)):
            row = jnp.broadcast_to(rows[order[p] : order[p] + 1, :], (16, LANES)).astype(half)
            me = jnp.full((16, LANES), p, half)
            for v in range(BAND // 16):
                first[v] = jnp.where(row == place[v], me, first[v])
            for v in range(p // 16 + 1):
                block = blocks[v]
                if v == p // 16:
                    block = jnp.where(place[0] < p % 16, block, jnp.full_like(block, -1))
                after[v] = jnp.where(row == block, me, after[v])
        after += [none] * ((LANES - N_REP) // 16)
        first = jnp.concatenate(first, axis=0).astype(jnp.float32).T.astype(jnp.int32)
        hop = jnp.concatenate(after, axis=0).astype(jnp.float32).T.astype(jnp.int32)
        hop2 = jnp.take_along_axis(hop, hop, axis=1)
        hop4 = jnp.take_along_axis(hop2, hop2, axis=1)
        hop8 = jnp.take_along_axis(hop4, hop4, axis=1)
        out[pl.ds(at, LANES), :] = hop | (hop2 << 7) | (hop4 << 14) | (first << 21)
        least = jnp.min(hop8.reshape(LANES // 8, 8, LANES), axis=0)
        deep[step] = jnp.where(jnp.min(least.astype(jnp.float32)) < NONE, 1, 0)
        return carry

    lax.fori_loop(0, chosen.shape[1] // LANES, one, 0)


def chain_sums(values, packed, levels):
    pad = jnp.zeros((LANES - N_REP, LANES), jnp.float32)
    total = jnp.concatenate([values, pad], axis=0).T
    for shift in (0, 7, 14):
        hop = (packed >> shift) & 127
        total = total + jnp.take_along_axis(total, hop, axis=1)
    for _ in range(levels):
        hop = jnp.take_along_axis(hop, hop, axis=1)
        total = total + jnp.take_along_axis(total, hop, axis=1)
    return jnp.take_along_axis(total, packed >> 21, axis=1)


def sum_kernel(top_deep, low_deep, values, top_table, low_table, out, energy, acc):
    step = pl.program_id(0)
    n = values.shape[1] // LANES
    upper = step < GROUPS // n

    @pl.when(step == 0)
    def _():
        acc[...] = jnp.zeros_like(acc)

    for s in range(n):
        at = slice(LANES * s, LANES * s + LANES)
        packed = jnp.where(upper, top_table[at, :], low_table[at, :])
        out[at, :] = chain_sums(values[:, at], packed, 0)

    def long_chains(s, carry):
        pair = step * n + s
        flag = jnp.where(upper, top_deep[jnp.minimum(pair, GROUPS - 1)], low_deep[jnp.maximum(pair - GROUPS, 0)])

        @pl.when(flag > 0)
        def _():
            at = pl.ds(pl.multiple_of(s * LANES, LANES), LANES)
            packed = jnp.where(upper, top_table[at, :], low_table[at, :])
            out[at, :] = chain_sums(values[:, at], packed, 4)

        return carry

    lax.fori_loop(0, n, long_chains, 0)
    summed = out[...]
    acc[...] += jnp.sum((summed * summed).reshape(LANES // 8 * n, 8, LANES), axis=0)

    @pl.when(step == pl.num_programs(0) - 1)
    def _():
        energy[...] = jnp.broadcast_to(acc[...][None], energy.shape)


def decode_kernel(summed, right, left, out, wide):
    wide[...] = times(summed[...], right)
    low = iota((TOPK, LANES), 1) < TILE
    for g in range(summed.shape[0] // LANES):
        pieces = []
        for u in (0, 2 * TOPK):
            a = slice(LANES * g + u, LANES * g + u + TOPK)
            b = slice(LANES * g + u + TOPK, LANES * g + u + 2 * TOPK)
            top = jnp.where(low, wide[a, :LANES], wide[b, LANES:])
            bottom = jnp.where(low, wide[a, LANES:], wide[b, :LANES])
            pieces.append(jnp.concatenate([top, bottom], axis=0))
        out[:, 256 * g : 256 * g + 256] = times_left(left, jnp.concatenate(pieces, axis=1))


def update_kernel(weight, decoded, energy, out):
    scale = jnp.sqrt(jnp.sum(energy[...]) / (ROWS * COLS * N_TP) + EPS)
    out[...] = weight[...] - decoded[...] * (RATE / jnp.full((1, 1), scale))


def whole(shape):
    return pl.BlockSpec(shape, lambda *_: (0,) * len(shape))


def params():
    return pltpu.CompilerParams(vmem_limit_bytes=VMEM)


def cost(flops, moved):
    return pl.CostEstimate(flops=flops, bytes_accessed=moved, transcendentals=0)


def constants():
    table = dct()
    eye2, eye4 = np.eye(2), np.eye(4)
    left = two(np.kron(eye2, table))
    right = two(np.kron(eye4, table.T))
    left_back = two(np.kron(eye2, table.T))
    right_back = two(np.kron(eye4, table))
    m = np.arange(LANES)[:, None]
    spread = (m // TOPK == np.arange(256)[None, :] // TILE).astype(ml_dtypes.bfloat16)
    pair = np.kron(eye2, table)
    cross = np.roll(pair, TILE, axis=1)
    decode_right = two(np.concatenate([pair, cross], axis=1))
    decode_left = two(np.concatenate([table[0::2], table[1::2]], axis=0).T)
    return left, right, left_back, right_back, spread, decode_right, decode_left


def own_specs():
    return [
        pl.BlockSpec((1, ROWS, COLS // HALVES), lambda g, rep: (0, 0, g)),
        pl.BlockSpec((1, ROWS, COLS // HALVES), lambda g, rep: (0, 0, g)),
        pl.BlockSpec((1, 2, COLS // HALVES // 2), lambda g, rep: (rep[0], 0, g)),
        whole((2, ROWS, ROWS)),
        whole((2, 256, 256)),
        whole((LANES, 256)),
    ]


def on_device(momentum, grad, weight, indices):
    left, right, left_back, right_back, spread, decode_right, decode_left = constants()
    rep = lax.axis_index("rep").astype(jnp.int32).reshape(1)
    picked = pl.pallas_call(
        pick_kernel,
        out_shape=jax.ShapeDtypeStruct((ZQ * YQ, 2, COLS // 2), jnp.float32),
        grid_spec=pltpu.PrefetchScalarGridSpec(
            num_scalar_prefetch=1,
            grid=(HALVES,),
            in_specs=own_specs() + [whole((256, LANES))],
            out_specs=pl.BlockSpec((ZQ * YQ, 2, COLS // HALVES // 2), lambda g, rep: (0, 0, g)),
            scratch_shapes=[pltpu.VMEM((ROWS * GROUPS // HALVES, 256), jnp.float32)],
        ),
        compiler_params=params(),
        cost_estimate=cost(1 << 30, 3 << 20),
    )(rep, momentum, grad, indices, left, right, spread, spread.T)

    far = lax.all_to_all(picked, "rep", 0, 0, tiled=True, axis_index_groups=far_groups())
    moment_out = pl.pallas_call(
        residual_kernel,
        out_shape=jax.ShapeDtypeStruct(momentum.shape, jnp.float32),
        grid_spec=pltpu.PrefetchScalarGridSpec(
            num_scalar_prefetch=1,
            grid=(HALVES,),
            in_specs=own_specs() + [whole((2, ROWS, ROWS)), whole((2, 256, 256))],
            out_specs=pl.BlockSpec((1, ROWS, COLS // HALVES), lambda g, rep: (0, 0, g)),
            scratch_shapes=[pltpu.VMEM((ROWS * GROUPS // HALVES, 256), jnp.float32)],
        ),
        compiler_params=params(),
        cost_estimate=cost(1 << 31, 5 << 20),
    )(rep, momentum, grad, indices, left, right, spread, left_back, right_back)

    flat = indices.reshape(N_REP, COLS)
    tables, deeps = [], []
    for a in range(2):
        table, deep = pl.pallas_call(
            table_kernel,
            out_shape=(
                jax.ShapeDtypeStruct((COLS // 2, LANES), jnp.int32),
                jax.ShapeDtypeStruct((GROUPS,), jnp.int32),
            ),
            grid=(1,),
            in_specs=[pl.BlockSpec((N_REP, COLS // 2), lambda s, a=a: (0, a))],
            out_specs=(
                pl.BlockSpec((COLS // 2, LANES), lambda s: (0, 0)),
                pl.BlockSpec(memory_space=pltpu.SMEM),
            ),
            scratch_shapes=[pltpu.VMEM((N_REP, LANES), jnp.float32)],
            compiler_params=params(),
            cost_estimate=cost(10 << 30, 2 << 20),
        )(flat)
        tables.append(table)
        deeps.append(deep)

    far, moment_out, tables[0] = lax.optimization_barrier((far, moment_out, tables[0]))
    near = jnp.broadcast_to(far.reshape(1, ZQ * YQ, COLS), (ZR * YR, ZQ * YQ, COLS))
    every = lax.all_to_all(near, "rep", 0, 0, tiled=True, axis_index_groups=near_groups())
    every = every.reshape(N_REP, COLS)

    wide = 7
    steps = PAIRS // wide
    half = steps // 2
    summed, energy = pl.pallas_call(
        sum_kernel,
        out_shape=(
            jax.ShapeDtypeStruct((COLS, LANES), jnp.float32),
            jax.ShapeDtypeStruct((N_TP, 8, LANES), jnp.float32),
        ),
        grid_spec=pltpu.PrefetchScalarGridSpec(
            num_scalar_prefetch=2,
            grid=(steps,),
            in_specs=[
                pl.BlockSpec((N_REP, wide * LANES), lambda s, *_: (0, s)),
                pl.BlockSpec((wide * LANES, LANES), lambda s, *_: (jnp.minimum(s, half - 1), 0)),
                pl.BlockSpec((wide * LANES, LANES), lambda s, *_: (jnp.maximum(s - half, 0), 0)),
            ],
            out_specs=(
                pl.BlockSpec((wide * LANES, LANES), lambda s, *_: (s, 0)),
                pl.BlockSpec((N_TP, 8, LANES), lambda s, *_: (0, 0, 0)),
            ),
            scratch_shapes=[pltpu.VMEM((8, LANES), jnp.float32)],
        ),
        compiler_params=params(),
        cost_estimate=cost(6 << 30, 5 << 20),
    )(*deeps, every, *tables)

    energies = lax.all_to_all(energy, "tp", 0, 0, tiled=True)

    decoded = pl.pallas_call(
        decode_kernel,
        out_shape=jax.ShapeDtypeStruct((ROWS, COLS), jnp.float32),
        grid=(2,),
        in_specs=[
            pl.BlockSpec((COLS // 2, LANES), lambda s: (s, 0)),
            whole((2, LANES, 256)),
            whole((2, TILE, TILE)),
        ],
        out_specs=pl.BlockSpec((TILE, COLS), lambda s: (s, 0)),
        scratch_shapes=[pltpu.VMEM((COLS // 2, 256), jnp.float32)],
        compiler_params=params(),
        cost_estimate=cost(1 << 30, 4 << 20),
    )(summed, decode_right, decode_left)

    weight_out = pl.pallas_call(
        update_kernel,
        out_shape=jax.ShapeDtypeStruct((ROWS, COLS), jnp.float32),
        grid=(2,),
        in_specs=[
            pl.BlockSpec((ROWS // 2, COLS), lambda s: (s, 0)),
            pl.BlockSpec((ROWS // 2, COLS), lambda s: (s, 0)),
            whole((N_TP, 8, LANES)),
        ],
        out_specs=pl.BlockSpec((ROWS // 2, COLS), lambda s: (s, 0)),
        compiler_params=params(),
        cost_estimate=cost(1 << 20, 6 << 20),
    )(weight, decoded, energies)
    return moment_out, weight_out


def solution(mesh):
    in_specs = (P("rep", None, "tp"), P("rep", None, "tp"), P(None, "tp"), P(None, None, "tp"))
    out_specs = (P("rep", None, "tp"), P(None, "tp"))
    return jax.shard_map(
        on_device, mesh=mesh, in_specs=in_specs, out_specs=out_specs, check_vma=False
    )
```

time: 532 us -> 102 us (0.19)
  other arithmetic: 259 us -> 0 us
  local copies, waits for them, and re-layouts: 124 us -> 4.1 us
  waiting for transfers between devices: 84.6 us -> 10.8 us
  Pallas kernels: 0 us -> 55.2 us
  starting transfers between devices: 0.04 us -> 30.1 us
  matrix products: 25.5 us -> 0 us
  blocking collectives: 20.6 us -> 0 us
  between operations: 14.8 us -> 0.71 us
    reduce_sum x26 -> x0, other arithmetic: 159 us -> none  [the longest x24 154 us: spread_values(): placed = jnp.sum(jnp.where(matches, values[..., None], 0.0), axis=0)]
    all_gather x1 -> x0, waiting for transfers between devices: 84.6 us -> none  [on_device(): every = lax.all_gather(sent, 'rep', axis=0, tiled=True)]
    add x25 -> x0, other arithmetic: 70.8 us -> none  [the longest x24 69.2 us: accumulate(): return (carry + spread_values(group_values, group_chosen), None)]
    reshape x31 -> x0, local copies, waits for them, and re-layouts: 57.2 us -> none  [the longest x24 38.6 us: spread_values(): return placed.reshape(tile_rows, tile_cols, TOPK * band_width)]
    pallas_call x0 -> x7, Pallas kernels: none -> 55.2 us  [the longest x2 22.3 us: on_device(): pl.pallas_call(table_kernel, out_shape=(jax.ShapeDtypeStruct((COLS // 2,...]
    all_to_all x0 -> x3, starting transfers between devices: none -> 30.1 us  [the longest x1 20.4 us: on_device(): lax.all_to_all(picked, 'rep', 0, 0, tiled=True, axis_index_groups=far_gro...]
    broadcast_in_dim x27 -> x1, local copies, waits for them, and re-layouts: 29.5 us -> 1.21 us  [on_device(): jnp.broadcast_to(far.reshape(1, ZQ * YQ, COLS), (ZR * YR, ZQ * YQ, COLS))]
    sub x27 -> x0, other arithmetic: 27.9 us -> none  [the longest x25 22.9 us: lane_offsets(): return chosen - band_start]
  transfers between devices with their start and end apart: 1 -> 3, of which waited for: 1 -> 1; matrix products, arithmetic and copies ran while one was open for 7% -> 1% of each run, Pallas kernels for 0% -> 35%
where the time goes in v1:
time: 102 us; the launch traced here: 101 us
  Pallas kernels  55.2 us (54%)
  starting transfers between devices  30.1 us (30%)
  waiting for transfers between devices  10.8 us (11%)
  local copies, waits for them, and re-layouts  4.1 us (4%)
    pallas_call x2, Pallas kernels, on_device(): pl.pallas_call(table_kernel, out_shape=(jax.ShapeDtypeStruct((COLS // 2,...  22.3 us
    all_to_all x1, starting transfers between devices, on_device(): lax.all_to_all(picked, 'rep', 0, 0, tiled=True, axis_index_groups=far_gro...  20.4 us
    pallas_call x1, Pallas kernels, on_device(): pl.pallas_call(sum_kernel, out_shape=(jax.ShapeDtypeStruct((COLS, LANES),...  11.3 us
    all_to_all x1, waiting for transfers between devices, on_device(): lax.all_to_all(near, 'rep', 0, 0, tiled=True, axis_index_groups=near_grou...  10.8 us
    pallas_call x1, Pallas kernels, on_device(): pl.pallas_call(residual_kernel, out_shape=jax.ShapeDtypeStruct(momentum.s...  7.33 us
    all_to_all x1, starting transfers between devices, on_device(): energies = lax.all_to_all(energy, 'tp', 0, 0, tiled=True)  6.16 us
    pallas_call x1, Pallas kernels, on_device(): pl.pallas_call(pick_kernel, out_shape=jax.ShapeDtypeStruct((ZQ * YQ, 2, C...  5.65 us
    pallas_call x1, Pallas kernels, on_device(): pl.pallas_call(decode_kernel, out_shape=jax.ShapeDtypeStruct((ROWS, COLS)...  5.38 us
  transfers between devices with their start and end apart: 3, of which 1 were waited for; matrix products, arithmetic and copies ran while one was open for 1% of the time, Pallas kernels for 35%

profile of v1, /device:TPU:1, one launch (start us, length us, event | category | flops | bytes accessed | tf_op | source)
XLA Modules:
  0.0 101.1 jit_solution(13815667074244310064)
XLA Ops:
  0.6 0.0 copy-start
  0.7 5.6 %shard_map.131 = f32[16,2,1792]{2,1,0:T(2,128)} custom-call(s32[1]{0:T(128)} %bitcast.rep, f32[1,128,3584]{2,1,0:T(8,128)} %momentum.3, bf16[1,128,3584]{2,1,0:T(8,128)(2,1)} %grad.3, s32[96,2,1792]{2,1,0:T(2,128)} %chosen.3, bf16[2,128,128]{2,1,0:T(8,128)(2,1)} %constant.21.clone.left, bf16[2,256,256]{2,1,0:T(8,128)(2,1)} %constant.22.clone.right, ...), custom_call_target="tpu_custom_call" | custom-call | flops 1073741824 | bytes 3145728 | tf_op jit(solution)/shard_map/pallas_call | solution.py:297
  6.3 20.4 %all-to-all-start = ((f32[16,2,1792]{2,1,0:T(2,128)}), f32[16,2,1792]{2,1,0:T(2,128)S(1)}, u32[]{:S(2)}, u32[]{:S(2)}) async-start(f32[16,2,1792]{2,1,0:T(2,128)} %shard_map.131), calls=%async_computation | async-start | bytes 458752 | tf_op jit(solution)/shard_map/all_to_all | solution.py:311
  26.7 0.0 copy-done
  26.7 1.2 %copy.14 = s32[12,8,2,1792]{3,1,2,0:T(8,128)} copy(s32[12,8,2,1792]{3,2,1,0:T(2,128)S(1)} %bitcast.6) | data formatting | bytes 2752512
  27.9 7.3 %shard_map.132 = f32[1,128,3584]{2,1,0:T(8,128)} custom-call(s32[1]{0:T(128)} %bitcast.rep, f32[1,128,3584]{2,1,0:T(8,128)} %momentum.3, bf16[1,128,3584]{2,1,0:T(8,128)(2,1)} %grad.3, s32[96,2,1792]{2,1,0:T(2,128)} %chosen.3, bf16[2,128,128]{2,1,0:T(8,128)(2,1)} %constant.21.clone.left, bf16[2,256,256]{2,1,0:T(8,128)(2,1)} %constant.22.clone.right, ...), custom_call_target="tpu_custom_call" | custom-call | flops 2147483648 | bytes 5242880 | tf_op jit(solution)/shard_map/pallas_call | solution.py:312
  35.2 11.1 %shard_map.133 = (s32[1792,128]{1,0:T(8,128)}, s32[14]{0:T(128)}) custom-call(s32[96,3584]{1,0:T(8,128)} %bitcast.7), custom_call_target="tpu_custom_call" | custom-call | flops 10737418240 | bytes 2097152 | tf_op jit(solution)/shard_map/pallas_call | solution.py:329
  46.4 0.0 all-to-all-done
  46.4 1.2 %broadcast_in_dim.8 = f32[6,16,3584]{2,1,0:T(8,128)} broadcast(f32[16,3584]{1,0:T(8,128)S(1)} %bitcast.10), dimensions={1,2} | broadcast | bytes 1605632 | tf_op jit(solution)/shard_map/broadcast_in_dim | solution.py:349
  47.6 3.6 %all-to-all-start.1 = ((f32[6,16,3584]{2,1,0:T(8,128)}), f32[6,16,3584]{2,1,0:T(8,128)S(1)}, u32[]{:S(2)}, u32[]{:S(2)}) async-start(f32[6,16,3584]{2,1,0:T(8,128)} %broadcast_in_dim.8), calls=%async_computation.1 | async-start | bytes 2752512 | tf_op jit(solution)/shard_map/all_to_all | solution.py:350
  51.2 11.2 %shard_map.134 = (s32[1792,128]{1,0:T(8,128)}, s32[14]{0:T(128)}) custom-call(s32[96,3584]{1,0:T(8,128)} %bitcast.8), custom_call_target="tpu_custom_call" | custom-call | flops 10737418240 | bytes 2097152 | tf_op jit(solution)/shard_map/pallas_call | solution.py:329
  62.4 10.8 %all-to-all-done.1 = f32[6,16,3584]{2,1,0:T(8,128)S(1)} async-done(((f32[6,16,3584]{2,1,0:T(8,128)}), f32[6,16,3584]{2,1,0:T(8,128)S(1)}, u32[]{:S(2)}, u32[]{:S(2)}) %all-to-all-start.1) | async-done | bytes 1376288 | tf_op jit(solution)/shard_map/all_to_all | solution.py:350
  73.2 0.0 copy-start.1
  73.2 1.1 %copy-done.1 = f32[6,16,3584]{2,1,0:T(8,128)} copy-done((f32[6,16,3584]{2,1,0:T(8,128)}, f32[6,16,3584]{2,1,0:T(8,128)S(1)}, u32[]{:S(2)}) %copy-start.1) | copy-done | bytes 1376280
  74.3 11.3 %shard_map.135 = (f32[3584,128]{1,0:T(8,128)}, f32[8,8,128]{2,1,0:T(8,128)}) custom-call(s32[14]{0:T(128)} %get-tuple-element.13.top_deep, s32[14]{0:T(128)} %get-tuple-element.14.low_deep, f32[96,3584]{1,0:T(8,128)} %bitcast.9, s32[1792,128]{1,0:T(8,128)} %get-tuple-element.16.top_table, s32[1792,128]{1,0:T(8,128)} %get-tuple-element.17.low_table), custom_call_target="tpu_custom_call" | custom-call | flops 6442450944 | bytes 5242880 | tf_op jit(solution)/shard_map/pallas_call | solution.py:356
  85.6 6.2 %all-to-all-start.2 = ((f32[8,8,128]{2,1,0:T(8,128)}), f32[8,8,128]{2,1,0:T(8,128)S(1)}, u32[]{:S(2)}, u32[]{:S(2)}) async-start(f32[8,8,128]{2,1,0:T(8,128)} %get-tuple-element.19), calls=%async_computation.2 | async-start | bytes 65536 | tf_op jit(solution)/shard_map/all_to_all | solution.py:380
  91.8 5.4 %shard_map.136.decoded = f32[128,3584]{1,0:T(8,128)} custom-call(f32[3584,128]{1,0:T(8,128)} %get-tuple-element.18.summed, bf16[2,128,256]{2,1,0:T(8,128)(2,1)} %constant.27.clone.right, bf16[2,64,64]{2,1,0:T(8,128)(2,1)} %constant.28.clone.left), custom_call_target="tpu_custom_call" | custom-call | flops 1073741824 | bytes 4194304 | tf_op jit(solution)/shard_map/pallas_call | solution.py:382
  97.2 0.0 all-to-all-done.2.energy
  97.2 0.0 copy-start.2
  97.2 0.6 copy-done.2
  97.8 3.3 %shard_map.137 = f32[128,3584]{1,0:T(8,128)} custom-call(f32[128,3584]{1,0:T(8,128)} %weight.1, f32[128,3584]{1,0:T(8,128)} %shard_map.136.decoded, f32[8,8,128]{2,1,0:T(8,128)} %copy-done.2), custom_call_target="tpu_custom_call" | custom-call | flops 1048576 | bytes 6291456 | tf_op jit(solution)/shard_map/pallas_call | solution.py:397
  (1 shorter events, 0.0 us)
Async XLA Ops:
  0.6 26.1 %copy-start = (s32[96,2,1792]{2,1,0:T(2,128)S(1)}, s32[96,2,1792]{2,1,0:T(2,128)}, u32[]{:S(2)}) copy-start(s32[96,2,1792]{2,1,0:T(2,128)} %chosen.3) | copy-start | bytes 4128772
  6.3 40.1 %all-to-all-start = ((f32[16,2,1792]{2,1,0:T(2,128)}), f32[16,2,1792]{2,1,0:T(2,128)S(1)}, u32[]{:S(2)}, u32[]{:S(2)}) async-start(f32[16,2,1792]{2,1,0:T(2,128)} %shard_map.131), calls=%async_computation | async-start | bytes 458752 | tf_op jit(solution)/shard_map/all_to_all | solution.py:311
  47.6 25.6 %all-to-all-start.1 = ((f32[6,16,3584]{2,1,0:T(8,128)}), f32[6,16,3584]{2,1,0:T(8,128)S(1)}, u32[]{:S(2)}, u32[]{:S(2)}) async-start(f32[6,16,3584]{2,1,0:T(8,128)} %broadcast_in_dim.8), calls=%async_computation.1 | async-start | bytes 2752512 | tf_op jit(solution)/shard_map/all_to_all | solution.py:350
  73.2 1.1 %copy-start.1 = (f32[6,16,3584]{2,1,0:T(8,128)}, f32[6,16,3584]{2,1,0:T(8,128)S(1)}, u32[]{:S(2)}) copy-start(f32[6,16,3584]{2,1,0:T(8,128)S(1)} %all-to-all-done.1) | copy-start | bytes 4128772
  85.6 11.5 %all-to-all-start.2 = ((f32[8,8,128]{2,1,0:T(8,128)}), f32[8,8,128]{2,1,0:T(8,128)S(1)}, u32[]{:S(2)}, u32[]{:S(2)}) async-start(f32[8,8,128]{2,1,0:T(8,128)} %get-tuple-element.19), calls=%async_computation.2 | async-start | bytes 65536 | tf_op jit(solution)/shard_map/all_to_all | solution.py:380
  97.2 0.6 copy-start.2

commit v2 on v1

--- a/solution.py
+++ b/solution.py
@@ -1,3 +1,5 @@
+import functools
+
 import jax
 import jax.numpy as jnp
 import ml_dtypes
@@ -24,6 +26,8 @@
 NONE = 127
 VMEM = 60 << 20
 HALVES = 2
+CHUNK = 7
+EARLY = 7
 
 Z, Y = 12, 8
 ZR, YR = 3, 2
@@ -85,10 +89,6 @@
 
 def iota(shape, dim):
     return lax.broadcasted_iota(jnp.int32, shape, dim)
-
-
-def stack(ref, n, width, axis=0):
-    return jnp.concatenate([ref[:, width * g : width * g + width] for g in range(n)], axis=axis)
 
 
 def kept_coefficients(momentum, grad, chosen, left, right, spread, wide):
@@ -146,7 +146,11 @@
         out[0, :, c] = decayed - back[ROWS * g : ROWS * g + ROWS]
 
 
-def table_kernel(chosen, out, deep, rows):
+def table_kernel(start, count, indices, out, deep, rows, chosen, sem):
+    columns = slice(start * LANES, (start + count) * LANES)
+    load = pltpu.make_async_copy(indices.at[:, columns], chosen, sem)
+    load.start()
+    load.wait()
     half = jnp.bfloat16
     order = replica_at()
 
@@ -198,35 +202,55 @@
     return jnp.take_along_axis(total, packed >> 21, axis=1)
 
 
-def sum_kernel(top_deep, low_deep, values, top_table, low_table, out, energy, acc):
+def sum_kernel(deep0, deep1, values, table0, table1, out, energy, acc):
     step = pl.program_id(0)
-    n = values.shape[1] // LANES
-    upper = step < GROUPS // n
+    early = step < EARLY // CHUNK
 
     @pl.when(step == 0)
     def _():
         acc[...] = jnp.zeros_like(acc)
 
-    for s in range(n):
-        at = slice(LANES * s, LANES * s + LANES)
-        packed = jnp.where(upper, top_table[at, :], low_table[at, :])
-        out[at, :] = chain_sums(values[:, at], packed, 0)
-
-    def long_chains(s, carry):
-        pair = step * n + s
-        flag = jnp.where(upper, top_deep[jnp.minimum(pair, GROUPS - 1)], low_deep[jnp.maximum(pair - GROUPS, 0)])
-
-        @pl.when(flag > 0)
-        def _():
-            at = pl.ds(pl.multiple_of(s * LANES, LANES), LANES)
-            packed = jnp.where(upper, top_table[at, :], low_table[at, :])
-            out[at, :] = chain_sums(values[:, at], packed, 4)
-
-        return carry
-
-    lax.fori_loop(0, n, long_chains, 0)
-    summed = out[...]
-    acc[...] += jnp.sum((summed * summed).reshape(LANES // 8 * n, 8, LANES), axis=0)
+    def run():
+        total = jnp.zeros((8, LANES), jnp.float32)
+        for s in range(CHUNK):
+            at = slice(LANES * s, LANES * s + LANES)
+            packed = jnp.where(early, table0[at, :], table1[at, :])
+            summed = chain_sums(values[:, at], packed, 0)
+            out[at, :] = summed
+            total += jnp.sum((summed * summed).reshape(LANES // 8, 8, LANES), axis=0)
+        acc[...] += total
+
+    flag = jnp.int32(0)
+    for s in range(CHUNK):
+        pair = step * CHUNK + s
+        late = deep1[jnp.maximum(pair - EARLY, 0)]
+        flag = jnp.maximum(flag, jnp.where(early, deep0[jnp.minimum(pair, EARLY - 1)], late))
+
+    @pl.when(flag == 0)
+    def _():
+        run()
+
+    @pl.when(flag > 0)
+    def _():
+        before = acc[...]
+        run()
+
+        def long_chains(s, carry):
+            pair = step * CHUNK + s
+            late = deep1[jnp.maximum(pair - EARLY, 0)]
+
+            @pl.when(jnp.where(early, deep0[jnp.minimum(pair, EARLY - 1)], late) > 0)
+            def _():
+                at = pl.ds(pl.multiple_of(s * LANES, LANES), LANES)
+                packed = jnp.where(early, table0[at, :], table1[at, :])
+                out[at, :] = chain_sums(values[:, at], packed, 4)
+
+            return carry
+
+        lax.fori_loop(0, CHUNK, long_chains, 0)
+        summed = out[...]
+        again = jnp.sum((summed * summed).reshape(LANES // 8 * CHUNK, 8, LANES), axis=0)
+        acc[...] = before + again
 
     @pl.when(step == pl.num_programs(0) - 1)
     def _():
@@ -256,8 +280,8 @@
     return pl.BlockSpec(shape, lambda *_: (0,) * len(shape))
 
 
-def params():
-    return pltpu.CompilerParams(vmem_limit_bytes=VMEM)
+def params(size=VMEM):
+    return pltpu.CompilerParams(vmem_limit_bytes=size)
 
 
 def cost(flops, moved):
@@ -323,24 +347,29 @@
         cost_estimate=cost(1 << 31, 5 << 20),
     )(rep, momentum, grad, indices, left, right, spread, left_back, right_back)
 
+    any_space = pl.BlockSpec(memory_space=pl.ANY)
     flat = indices.reshape(N_REP, COLS)
     tables, deeps = [], []
-    for a in range(2):
+    for first, count in ((0, EARLY), (EARLY, PAIRS - EARLY)):
         table, deep = pl.pallas_call(
-            table_kernel,
+            functools.partial(table_kernel, first, count),
             out_shape=(
-                jax.ShapeDtypeStruct((COLS // 2, LANES), jnp.int32),
-                jax.ShapeDtypeStruct((GROUPS,), jnp.int32),
+                jax.ShapeDtypeStruct((count * LANES, LANES), jnp.int32),
+                jax.ShapeDtypeStruct((count,), jnp.int32),
             ),
             grid=(1,),
-            in_specs=[pl.BlockSpec((N_REP, COLS // 2), lambda s, a=a: (0, a))],
+            in_specs=[any_space],
             out_specs=(
-                pl.BlockSpec((COLS // 2, LANES), lambda s: (0, 0)),
+                pl.BlockSpec((count * LANES, LANES), lambda s: (0, 0)),
                 pl.BlockSpec(memory_space=pltpu.SMEM),
             ),
-            scratch_shapes=[pltpu.VMEM((N_REP, LANES), jnp.float32)],
-            compiler_params=params(),
-            cost_estimate=cost(10 << 30, 2 << 20),
+            scratch_shapes=[
+                pltpu.VMEM((N_REP, LANES), jnp.float32),
+                pltpu.VMEM((N_REP, count * LANES), jnp.int32),
+                pltpu.SemaphoreType.DMA,
+            ],
+            compiler_params=params(60 << 20),
+            cost_estimate=cost(count << 30, 2 << 20),
         )(flat)
         tables.append(table)
         deeps.append(deep)
@@ -350,9 +379,6 @@
     every = lax.all_to_all(near, "rep", 0, 0, tiled=True, axis_index_groups=near_groups())
     every = every.reshape(N_REP, COLS)
 
-    wide = 7
-    steps = PAIRS // wide
-    half = steps // 2
     summed, energy = pl.pallas_call(
         sum_kernel,
         out_shape=(
@@ -361,19 +387,19 @@
         ),
         grid_spec=pltpu.PrefetchScalarGridSpec(
             num_scalar_prefetch=2,
-            grid=(steps,),
+            grid=(PAIRS // CHUNK,),
             in_specs=[
-                pl.BlockSpec((N_REP, wide * LANES), lambda s, *_: (0, s)),
-                pl.BlockSpec((wide * LANES, LANES), lambda s, *_: (jnp.minimum(s, half - 1), 0)),
-                pl.BlockSpec((wide * LANES, LANES), lambda s, *_: (jnp.maximum(s - half, 0), 0)),
+                pl.BlockSpec((N_REP, CHUNK * LANES), lambda s, *_: (0, s)),
+                pl.BlockSpec((CHUNK * LANES, LANES), lambda s, *_: (jnp.minimum(s, EARLY // CHUNK - 1), 0)),
+                pl.BlockSpec((CHUNK * LANES, LANES), lambda s, *_: (jnp.maximum(s - EARLY // CHUNK, 0), 0)),
             ],
             out_specs=(
-                pl.BlockSpec((wide * LANES, LANES), lambda s, *_: (s, 0)),
-                pl.BlockSpec((N_TP, 8, LANES), lambda s, *_: (0, 0, 0)),
+                pl.BlockSpec((CHUNK * LANES, LANES), lambda s, *_: (s, 0)),
+                whole((N_TP, 8, LANES)),
             ),
             scratch_shapes=[pltpu.VMEM((8, LANES), jnp.float32)],
         ),
-        compiler_params=params(),
+        compiler_params=params(60 << 20),
         cost_estimate=cost(6 << 30, 5 << 20),
     )(*deeps, every, *tables)
 

time: 102 us -> 97 us (0.951)
  waiting for transfers between devices: 10.8 us -> 4.03 us
  starting transfers between devices: 30.1 us -> 33.1 us
    all_to_all x1, waiting for transfers between devices: 10.8 us -> 4.02 us  [on_device(): lax.all_to_all(near, 'rep', 0, 0, tiled=True, axis_index_groups=near_grou...]
    all_to_all x1, starting transfers between devices: 6.16 us -> 8.27 us  [on_device(): energies = lax.all_to_all(energy, 'tp', 0, 0, tiled=True)]
  transfers between devices with their start and end apart: 3 -> 3, of which waited for: 1 -> 1; matrix products, arithmetic and copies ran while one was open for 1% -> 1% of each run, Pallas kernels for 35% -> 36%
where the time goes in v2:
time: 97 us; the launch traced here: 96.5 us
  Pallas kernels  54.6 us (56%)
  starting transfers between devices  33.1 us (34%)
  local copies, waits for them, and re-layouts  4.09 us (4%)
  waiting for transfers between devices  4.03 us (4%)
    pallas_call x2, Pallas kernels, on_device(): pl.pallas_call(functools.partial(table_kernel, first, count), out_shape=(...  22.3 us
    all_to_all x1, starting transfers between devices, on_device(): lax.all_to_all(picked, 'rep', 0, 0, tiled=True, axis_index_groups=far_gro...  20.4 us
    pallas_call x1, Pallas kernels, on_device(): pl.pallas_call(sum_kernel, out_shape=(jax.ShapeDtypeStruct((COLS, LANES),...  10.6 us
    all_to_all x1, starting transfers between devices, on_device(): energies = lax.all_to_all(energy, 'tp', 0, 0, tiled=True)  8.27 us
    pallas_call x1, Pallas kernels, on_device(): pl.pallas_call(residual_kernel, out_shape=jax.ShapeDtypeStruct(momentum.s...  7.33 us
    pallas_call x1, Pallas kernels, on_device(): pl.pallas_call(pick_kernel, out_shape=jax.ShapeDtypeStruct((ZQ * YQ, 2, C...  5.65 us
    pallas_call x1, Pallas kernels, on_device(): pl.pallas_call(decode_kernel, out_shape=jax.ShapeDtypeStruct((ROWS, COLS)...  5.38 us
    all_to_all x1, starting transfers between devices, on_device(): lax.all_to_all(near, 'rep', 0, 0, tiled=True, axis_index_groups=near_grou...  4.42 us
  transfers between devices with their start and end apart: 3, of which 1 were waited for; matrix products, arithmetic and copies ran while one was open for 1% of the time, Pallas kernels for 36%

profile of v2, /device:TPU:1, one launch (start us, length us, event | category | flops | bytes accessed | tf_op | source)
XLA Modules:
  0.0 96.5 jit_solution(14831490450817723411)
XLA Ops:
  0.6 0.0 copy-start
  0.7 5.6 %shard_map.131 = f32[16,2,1792]{2,1,0:T(2,128)} custom-call(s32[1]{0:T(128)} %bitcast.rep, f32[1,128,3584]{2,1,0:T(8,128)} %momentum.3, bf16[1,128,3584]{2,1,0:T(8,128)(2,1)} %grad.3, s32[96,2,1792]{2,1,0:T(2,128)} %chosen.3, bf16[2,128,128]{2,1,0:T(8,128)(2,1)} %constant.21.clone.left, bf16[2,256,256]{2,1,0:T(8,128)(2,1)} %constant.22.clone.right, ...), custom_call_target="tpu_custom_call" | custom-call | flops 1073741824 | bytes 3145728 | tf_op jit(solution)/shard_map/pallas_call | solution.py:321
  6.3 20.4 %all-to-all-start = ((f32[16,2,1792]{2,1,0:T(2,128)}), f32[16,2,1792]{2,1,0:T(2,128)S(1)}, u32[]{:S(2)}, u32[]{:S(2)}) async-start(f32[16,2,1792]{2,1,0:T(2,128)} %shard_map.131), calls=%async_computation | async-start | bytes 458752 | tf_op jit(solution)/shard_map/all_to_all | solution.py:335
  26.7 0.0 copy-done
  26.7 1.2 %copy.14 = s32[12,8,2,1792]{3,1,2,0:T(8,128)} copy(s32[12,8,2,1792]{3,2,1,0:T(2,128)S(1)} %bitcast.6) | data formatting | bytes 2752512
  27.9 7.3 %shard_map.132 = f32[1,128,3584]{2,1,0:T(8,128)} custom-call(s32[1]{0:T(128)} %bitcast.rep, f32[1,128,3584]{2,1,0:T(8,128)} %momentum.3, bf16[1,128,3584]{2,1,0:T(8,128)(2,1)} %grad.3, s32[96,2,1792]{2,1,0:T(2,128)} %chosen.3, bf16[2,128,128]{2,1,0:T(8,128)(2,1)} %constant.21.clone.left, bf16[2,256,256]{2,1,0:T(8,128)(2,1)} %constant.22.clone.right, ...), custom_call_target="tpu_custom_call" | custom-call | flops 2147483648 | bytes 5242880 | tf_op jit(solution)/shard_map/pallas_call | solution.py:336
  35.2 6.3 %shard_map.133 = (s32[896,128]{1,0:T(8,128)}, s32[7]{0:T(128)}) custom-call(s32[96,3584]{1,0:T(8,128)} %bitcast.7), custom_call_target="tpu_custom_call" | custom-call | flops 7516192768 | bytes 2097152 | tf_op jit(solution)/shard_map/pallas_call | solution.py:354
  41.6 0.0 all-to-all-done
  41.6 1.2 %broadcast_in_dim.8 = f32[6,16,3584]{2,1,0:T(8,128)} broadcast(f32[16,3584]{1,0:T(8,128)S(1)} %bitcast.10), dimensions={1,2} | broadcast | bytes 1605632 | tf_op jit(solution)/shard_map/broadcast_in_dim | solution.py:378
  42.8 4.4 %all-to-all-start.1 = ((f32[6,16,3584]{2,1,0:T(8,128)}), f32[6,16,3584]{2,1,0:T(8,128)S(1)}, u32[]{:S(2)}, u32[]{:S(2)}) async-start(f32[6,16,3584]{2,1,0:T(8,128)} %broadcast_in_dim.8), calls=%async_computation.1 | async-start | bytes 2752512 | tf_op jit(solution)/shard_map/all_to_all | solution.py:379
  47.2 16.0 %shard_map.134 = (s32[2688,128]{1,0:T(8,128)}, s32[21]{0:T(128)}) custom-call(s32[96,3584]{1,0:T(8,128)} %bitcast.8), custom_call_target="tpu_custom_call" | custom-call | flops 22548578304 | bytes 2097152 | tf_op jit(solution)/shard_map/pallas_call | solution.py:354
  63.3 4.0 %all-to-all-done.1 = f32[6,16,3584]{2,1,0:T(8,128)S(1)} async-done(((f32[6,16,3584]{2,1,0:T(8,128)}), f32[6,16,3584]{2,1,0:T(8,128)S(1)}, u32[]{:S(2)}, u32[]{:S(2)}) %all-to-all-start.1) | async-done | bytes 1376288 | tf_op jit(solution)/shard_map/all_to_all | solution.py:379
  67.3 0.0 copy-start.1
  67.3 1.1 %copy-done.1 = f32[6,16,3584]{2,1,0:T(8,128)} copy-done((f32[6,16,3584]{2,1,0:T(8,128)}, f32[6,16,3584]{2,1,0:T(8,128)S(1)}, u32[]{:S(2)}) %copy-start.1) | copy-done | bytes 1376280
  68.4 10.6 %shard_map.135 = (f32[3584,128]{1,0:T(8,128)}, f32[8,8,128]{2,1,0:T(8,128)}) custom-call(s32[7]{0:T(128)} %get-tuple-element.13.deep0, s32[21]{0:T(128)} %get-tuple-element.14.deep1, f32[96,3584]{1,0:T(8,128)} %bitcast.9, s32[896,128]{1,0:T(8,128)} %get-tuple-element.16.table0, s32[2688,128]{1,0:T(8,128)} %get-tuple-element.17.table1), custom_call_target="tpu_custom_call" | custom-call | flops 6442450944 | bytes 5242880 | tf_op jit(solution)/shard_map/pallas_call | solution.py:382
  79.0 8.3 %all-to-all-start.2 = ((f32[8,8,128]{2,1,0:T(8,128)}), f32[8,8,128]{2,1,0:T(8,128)S(1)}, u32[]{:S(2)}, u32[]{:S(2)}) async-start(f32[8,8,128]{2,1,0:T(8,128)} %get-tuple-element.19), calls=%async_computation.2 | async-start | bytes 65536 | tf_op jit(solution)/shard_map/all_to_all | solution.py:406
  87.2 5.4 %shard_map.136.decoded = f32[128,3584]{1,0:T(8,128)} custom-call(f32[3584,128]{1,0:T(8,128)} %get-tuple-element.18.summed, bf16[2,128,256]{2,1,0:T(8,128)(2,1)} %constant.27.clone.right, bf16[2,64,64]{2,1,0:T(8,128)(2,1)} %constant.28.clone.left), custom_call_target="tpu_custom_call" | custom-call | flops 1073741824 | bytes 4194304 | tf_op jit(solution)/shard_map/pallas_call | solution.py:408
  92.6 0.0 all-to-all-done.2.energy
  92.6 0.0 copy-start.2
  92.6 0.6 copy-done.2
  93.2 3.3 %shard_map.137 = f32[128,3584]{1,0:T(8,128)} custom-call(f32[128,3584]{1,0:T(8,128)} %weight.1, f32[128,3584]{1,0:T(8,128)} %shard_map.136.decoded, f32[8,8,128]{2,1,0:T(8,128)} %copy-done.2), custom_call_target="tpu_custom_call" | custom-call | flops 1048576 | bytes 6291456 | tf_op jit(solution)/shard_map/pallas_call | solution.py:423
  (1 shorter events, 0.0 us)
Async XLA Ops:
  0.6 26.1 %copy-start = (s32[96,2,1792]{2,1,0:T(2,128)S(1)}, s32[96,2,1792]{2,1,0:T(2,128)}, u32[]{:S(2)}) copy-start(s32[96,2,1792]{2,1,0:T(2,128)} %chosen.3) | copy-start | bytes 4128772
  6.3 35.3 %all-to-all-start = ((f32[16,2,1792]{2,1,0:T(2,128)}), f32[16,2,1792]{2,1,0:T(2,128)S(1)}, u32[]{:S(2)}, u32[]{:S(2)}) async-start(f32[16,2,1792]{2,1,0:T(2,128)} %shard_map.131), calls=%async_computation | async-start | bytes 458752 | tf_op jit(solution)/shard_map/all_to_all | solution.py:335
  42.8 24.4 %all-to-all-start.1 = ((f32[6,16,3584]{2,1,0:T(8,128)}), f32[6,16,3584]{2,1,0:T(8,128)S(1)}, u32[]{:S(2)}, u32[]{:S(2)}) async-start(f32[6,16,3584]{2,1,0:T(8,128)} %broadcast_in_dim.8), calls=%async_computation.1 | async-start | bytes 2752512 | tf_op jit(solution)/shard_map/all_to_all | solution.py:379
  67.3 1.1 %copy-start.1 = (f32[6,16,3584]{2,1,0:T(8,128)}, f32[6,16,3584]{2,1,0:T(8,128)S(1)}, u32[]{:S(2)}) copy-start(f32[6,16,3584]{2,1,0:T(8,128)S(1)} %all-to-all-done.1) | copy-start | bytes 4128772
  79.0 13.7 %all-to-all-start.2 = ((f32[8,8,128]{2,1,0:T(8,128)}), f32[8,8,128]{2,1,0:T(8,128)S(1)}, u32[]{:S(2)}, u32[]{:S(2)}) async-start(f32[8,8,128]{2,1,0:T(8,128)} %get-tuple-element.19), calls=%async_computation.2 | async-start | bytes 65536 | tf_op jit(solution)/shard_map/all_to_all | solution.py:406
  92.6 0.6 copy-start.2

commit v3 on v2

--- a/solution.py
+++ b/solution.py
@@ -382,7 +382,7 @@
     summed, energy = pl.pallas_call(
         sum_kernel,
         out_shape=(
-            jax.ShapeDtypeStruct((COLS, LANES), jnp.float32),
+            pltpu.HBM((COLS, LANES), jnp.float32),
             jax.ShapeDtypeStruct((N_TP, 8, LANES), jnp.float32),
         ),
         grid_spec=pltpu.PrefetchScalarGridSpec(
@@ -399,7 +399,7 @@
             ),
             scratch_shapes=[pltpu.VMEM((8, LANES), jnp.float32)],
         ),
-        compiler_params=params(60 << 20),
+        compiler_params=params(40 << 20),
         cost_estimate=cost(6 << 30, 5 << 20),
     )(*deeps, every, *tables)
 

time: 97 us -> 96.5 us (level)
  Pallas kernels: 54.6 us -> 53.3 us
    pallas_call x1, Pallas kernels: 10.6 us -> 9.29 us  [on_device(): pl.pallas_call(sum_kernel, out_shape=(pltpu.HBM((COLS, LANES), jnp.float3...]
    unnamed x8 -> x14, local copies, waits for them, and re-layouts: 2.88 us -> 3.75 us
  transfers between devices with their start and end apart: 3 -> 3, of which waited for: 1 -> 1; matrix products, arithmetic and copies ran while one was open for 1% -> 1% of each run, Pallas kernels for 36% -> 37%
where the time goes in v3:
time: 96.5 us; the launch traced here: 96.1 us
  Pallas kernels  53.3 us (55%)
  starting transfers between devices  33.1 us (34%)
  local copies, waits for them, and re-layouts  4.95 us (5%)
  waiting for transfers between devices  3.94 us (4%)
    pallas_call x2, Pallas kernels, on_device(): pl.pallas_call(functools.partial(table_kernel, first, count), out_shape=(...  22.4 us
    all_to_all x1, starting transfers between devices, on_device(): lax.all_to_all(picked, 'rep', 0, 0, tiled=True, axis_index_groups=far_gro...  20.4 us
    pallas_call x1, Pallas kernels, on_device(): pl.pallas_call(sum_kernel, out_shape=(pltpu.HBM((COLS, LANES), jnp.float3...  9.29 us
    all_to_all x1, starting transfers between devices, on_device(): energies = lax.all_to_all(energy, 'tp', 0, 0, tiled=True)  8.27 us
    pallas_call x1, Pallas kernels, on_device(): pl.pallas_call(residual_kernel, out_shape=jax.ShapeDtypeStruct(momentum.s...  7.34 us
    pallas_call x1, Pallas kernels, on_device(): pl.pallas_call(pick_kernel, out_shape=jax.ShapeDtypeStruct((ZQ * YQ, 2, C...  5.66 us
    pallas_call x1, Pallas kernels, on_device(): pl.pallas_call(decode_kernel, out_shape=jax.ShapeDtypeStruct((ROWS, COLS)...  5.4 us
    all_to_all x1, starting transfers between devices, on_device(): lax.all_to_all(near, 'rep', 0, 0, tiled=True, axis_index_groups=near_grou...  4.44 us
  transfers between devices with their start and end apart: 3, of which 1 were waited for; matrix products, arithmetic and copies ran while one was open for 1% of the time, Pallas kernels for 37%

profile of v3, /device:TPU:1, one launch (start us, length us, event | category | flops | bytes accessed | tf_op | source)
XLA Modules:
  0.0 96.1 jit_solution(3612826082458311919)
XLA Ops:
  0.6 0.0 copy-start.4
  0.7 5.7 %shard_map.131 = f32[16,2,1792]{2,1,0:T(2,128)} custom-call(s32[1]{0:T(128)} %bitcast.rep, f32[1,128,3584]{2,1,0:T(8,128)} %momentum.3, bf16[1,128,3584]{2,1,0:T(8,128)(2,1)} %grad.3, s32[96,2,1792]{2,1,0:T(2,128)} %chosen.3, bf16[2,128,128]{2,1,0:T(8,128)(2,1)} %constant.21.clone.left, bf16[2,256,256]{2,1,0:T(8,128)(2,1)} %constant.22.clone.right, ...), custom_call_target="tpu_custom_call" | custom-call | flops 1073741824 | bytes 3145728 | tf_op jit(solution)/shard_map/pallas_call | solution.py:321
  6.3 20.4 %all-to-all-start = ((f32[16,2,1792]{2,1,0:T(2,128)}), f32[16,2,1792]{2,1,0:T(2,128)S(1)}, u32[]{:S(2)}, u32[]{:S(2)}) async-start(f32[16,2,1792]{2,1,0:T(2,128)} %shard_map.131), calls=%async_computation | async-start | bytes 458752 | tf_op jit(solution)/shard_map/all_to_all | solution.py:335
  26.7 0.0 copy-done.4
  26.7 1.2 %copy.14 = s32[12,8,2,1792]{3,1,2,0:T(8,128)} copy(s32[12,8,2,1792]{3,2,1,0:T(2,128)S(1)} %bitcast.7) | data formatting | bytes 2752512
  27.9 7.3 %shard_map.132 = f32[1,128,3584]{2,1,0:T(8,128)} custom-call(s32[1]{0:T(128)} %bitcast.rep, f32[1,128,3584]{2,1,0:T(8,128)} %momentum.3, bf16[1,128,3584]{2,1,0:T(8,128)(2,1)} %grad.3, s32[96,2,1792]{2,1,0:T(2,128)} %chosen.3, bf16[2,128,128]{2,1,0:T(8,128)(2,1)} %constant.21.clone.left, bf16[2,256,256]{2,1,0:T(8,128)(2,1)} %constant.22.clone.right, ...), custom_call_target="tpu_custom_call" | custom-call | flops 2147483648 | bytes 5242880 | tf_op jit(solution)/shard_map/pallas_call | solution.py:336
  35.3 6.3 %shard_map.133 = (s32[896,128]{1,0:T(8,128)}, s32[7]{0:T(128)}) custom-call(s32[96,3584]{1,0:T(8,128)} %bitcast.8), custom_call_target="tpu_custom_call" | custom-call | flops 7516192768 | bytes 2097152 | tf_op jit(solution)/shard_map/pallas_call | solution.py:354
  41.6 0.0 all-to-all-done
  41.6 1.2 %broadcast_in_dim.8 = f32[6,16,3584]{2,1,0:T(8,128)} broadcast(f32[16,3584]{1,0:T(8,128)S(1)} %bitcast.10), dimensions={1,2} | broadcast | bytes 1605632 | tf_op jit(solution)/shard_map/broadcast_in_dim | solution.py:378
  42.8 4.4 %all-to-all-start.1 = ((f32[6,16,3584]{2,1,0:T(8,128)}), f32[6,16,3584]{2,1,0:T(8,128)S(1)}, u32[]{:S(2)}, u32[]{:S(2)}) async-start(f32[6,16,3584]{2,1,0:T(8,128)} %broadcast_in_dim.8), calls=%async_computation.1 | async-start | bytes 2752512 | tf_op jit(solution)/shard_map/all_to_all | solution.py:379
  47.3 0.0 copy-start.1
  47.3 0.0 copy-start.2
  47.3 16.1 %shard_map.134 = (s32[2688,128]{1,0:T(8,128)}, s32[21]{0:T(128)}) custom-call(s32[96,3584]{1,0:T(8,128)} %bitcast.9), custom_call_target="tpu_custom_call" | custom-call | flops 22548578304 | bytes 2097152 | tf_op jit(solution)/shard_map/pallas_call | solution.py:354
  63.3 3.9 %all-to-all-done.1 = f32[6,16,3584]{2,1,0:T(8,128)S(1)} async-done(((f32[6,16,3584]{2,1,0:T(8,128)}), f32[6,16,3584]{2,1,0:T(8,128)S(1)}, u32[]{:S(2)}, u32[]{:S(2)}) %all-to-all-start.1) | async-done | bytes 1376288 | tf_op jit(solution)/shard_map/all_to_all | solution.py:379
  67.3 0.0 copy-done.1
  67.3 0.0 copy-done.2
  67.3 0.0 copy-start
  67.3 1.3 %copy-done = s32[2688,128]{1,0:T(8,128)S(1)} copy-done((s32[2688,128]{1,0:T(8,128)S(1)}, s32[2688,128]{1,0:T(8,128)}, u32[]{:S(2)}) %copy-start) | copy-done | bytes 1376280
  68.6 0.0 copy-start.3
  68.6 0.6 copy-done.3
  69.2 9.3 %shard_map.135 = (f32[3584,128]{1,0:T(8,128)}, f32[8,8,128]{2,1,0:T(8,128)}) custom-call(s32[7]{0:T(128)S(1)} %copy-done.2, s32[21]{0:T(128)S(1)} %copy-done.3, f32[96,3584]{1,0:T(8,128)S(1)} %bitcast.6, s32[896,128]{1,0:T(8,128)S(1)} %copy-done.1, s32[2688,128]{1,0:T(8,128)S(1)} %copy-done), custom_call_target="tpu_custom_call" | custom-call | flops 6442450944 | bytes 5242880 | tf_op jit(solution)/shard_map/pallas_call | solution.py:382
  78.5 8.3 %all-to-all-start.2 = ((f32[8,8,128]{2,1,0:T(8,128)}), f32[8,8,128]{2,1,0:T(8,128)S(1)}, u32[]{:S(2)}, u32[]{:S(2)}) async-start(f32[8,8,128]{2,1,0:T(8,128)} %get-tuple-element.19), calls=%async_computation.2 | async-start | bytes 65536 | tf_op jit(solution)/shard_map/all_to_all | solution.py:406
  86.8 5.4 %shard_map.136.decoded = f32[128,3584]{1,0:T(8,128)} custom-call(f32[3584,128]{1,0:T(8,128)} %get-tuple-element.18.summed, bf16[2,128,256]{2,1,0:T(8,128)(2,1)} %constant.27.clone.right, bf16[2,64,64]{2,1,0:T(8,128)(2,1)} %constant.28.clone.left), custom_call_target="tpu_custom_call" | custom-call | flops 1073741824 | bytes 4194304 | tf_op jit(solution)/shard_map/pallas_call | solution.py:408
  92.2 0.0 all-to-all-done.2.energy
  92.2 0.0 copy-start.5
  92.2 0.6 copy-done.5
  92.8 3.3 %shard_map.137 = f32[128,3584]{1,0:T(8,128)} custom-call(f32[128,3584]{1,0:T(8,128)} %weight.1, f32[128,3584]{1,0:T(8,128)} %shard_map.136.decoded, f32[8,8,128]{2,1,0:T(8,128)} %copy-done.5), custom_call_target="tpu_custom_call" | custom-call | flops 1048576 | bytes 6291456 | tf_op jit(solution)/shard_map/pallas_call | solution.py:423
  (1 shorter events, 0.0 us)
Async XLA Ops:
  0.6 26.1 %copy-start.4 = (s32[96,2,1792]{2,1,0:T(2,128)S(1)}, s32[96,2,1792]{2,1,0:T(2,128)}, u32[]{:S(2)}) copy-start(s32[96,2,1792]{2,1,0:T(2,128)} %chosen.3) | copy-start | bytes 4128772
  6.3 35.3 %all-to-all-start = ((f32[16,2,1792]{2,1,0:T(2,128)}), f32[16,2,1792]{2,1,0:T(2,128)S(1)}, u32[]{:S(2)}, u32[]{:S(2)}) async-start(f32[16,2,1792]{2,1,0:T(2,128)} %shard_map.131), calls=%async_computation | async-start | bytes 458752 | tf_op jit(solution)/shard_map/all_to_all | solution.py:335
  42.8 24.5 %all-to-all-start.1 = ((f32[6,16,3584]{2,1,0:T(8,128)}), f32[6,16,3584]{2,1,0:T(8,128)S(1)}, u32[]{:S(2)}, u32[]{:S(2)}) async-start(f32[6,16,3584]{2,1,0:T(8,128)} %broadcast_in_dim.8), calls=%async_computation.1 | async-start | bytes 2752512 | tf_op jit(solution)/shard_map/all_to_all | solution.py:379
  47.3 20.0 %copy-start.1 = (s32[896,128]{1,0:T(8,128)S(1)}, s32[896,128]{1,0:T(8,128)}, u32[]{:S(2)}) copy-start(s32[896,128]{1,0:T(8,128)} %get-tuple-element.16.table0) | copy-start | bytes 1376260
  47.3 20.0 %copy-start.2 = (s32[7]{0:T(128)S(1)}, s32[7]{0:T(128)}, u32[]{:S(2)}) copy-start(s32[7]{0:T(128)} %get-tuple-element.13.deep0) | copy-start | bytes 88
  67.3 1.3 %copy-start = (s32[2688,128]{1,0:T(8,128)S(1)}, s32[2688,128]{1,0:T(8,128)}, u32[]{:S(2)}) copy-start(s32[2688,128]{1,0:T(8,128)} %get-tuple-element.17.table1) | copy-start | bytes 4128772
  68.6 0.6 copy-start.3
  78.5 13.7 %all-to-all-start.2 = ((f32[8,8,128]{2,1,0:T(8,128)}), f32[8,8,128]{2,1,0:T(8,128)S(1)}, u32[]{:S(2)}, u32[]{:S(2)}) async-start(f32[8,8,128]{2,1,0:T(8,128)} %get-tuple-element.19), calls=%async_computation.2 | async-start | bytes 65536 | tf_op jit(solution)/shard_map/all_to_all | solution.py:406
  92.2 0.6 copy-start.5

commit v4 on v3

--- a/solution.py
+++ b/solution.py
@@ -399,7 +399,7 @@
             ),
             scratch_shapes=[pltpu.VMEM((8, LANES), jnp.float32)],
         ),
-        compiler_params=params(40 << 20),
+        compiler_params=params(61341696),
         cost_estimate=cost(6 << 30, 5 << 20),
     )(*deeps, every, *tables)
 

time: 96.5 us -> 97 us (level)
  Pallas kernels: 53.3 us -> 54.6 us
    pallas_call x1, Pallas kernels: 9.29 us -> 10.6 us  [on_device(): pl.pallas_call(sum_kernel, out_shape=(pltpu.HBM((COLS, LANES), jnp.float3...]
    unnamed x14 -> x8, local copies, waits for them, and re-layouts: 3.75 us -> 2.88 us
  transfers between devices with their start and end apart: 3 -> 3, of which waited for: 1 -> 1; matrix products, arithmetic and copies ran while one was open for 1% -> 1% of each run, Pallas kernels for 37% -> 36%
where the time goes in v4:
time: 97 us; the launch traced here: 96.5 us
  Pallas kernels  54.6 us (56%)
  starting transfers between devices  33.1 us (34%)
  local copies, waits for them, and re-layouts  4.09 us (4%)
  waiting for transfers between devices  4.03 us (4%)
    pallas_call x2, Pallas kernels, on_device(): pl.pallas_call(functools.partial(table_kernel, first, count), out_shape=(...  22.3 us
    all_to_all x1, starting transfers between devices, on_device(): lax.all_to_all(picked, 'rep', 0, 0, tiled=True, axis_index_groups=far_gro...  20.4 us
    pallas_call x1, Pallas kernels, on_device(): pl.pallas_call(sum_kernel, out_shape=(pltpu.HBM((COLS, LANES), jnp.float3...  10.6 us
    all_to_all x1, starting transfers between devices, on_device(): energies = lax.all_to_all(energy, 'tp', 0, 0, tiled=True)  8.27 us
    pallas_call x1, Pallas kernels, on_device(): pl.pallas_call(residual_kernel, out_shape=jax.ShapeDtypeStruct(momentum.s...  7.33 us
    pallas_call x1, Pallas kernels, on_device(): pl.pallas_call(pick_kernel, out_shape=jax.ShapeDtypeStruct((ZQ * YQ, 2, C...  5.65 us
    pallas_call x1, Pallas kernels, on_device(): pl.pallas_call(decode_kernel, out_shape=jax.ShapeDtypeStruct((ROWS, COLS)...  5.38 us
    all_to_all x1, starting transfers between devices, on_device(): lax.all_to_all(near, 'rep', 0, 0, tiled=True, axis_index_groups=near_grou...  4.42 us
  transfers between devices with their start and end apart: 3, of which 1 were waited for; matrix products, arithmetic and copies ran while one was open for 1% of the time, Pallas kernels for 36%

profile of v4, /device:TPU:1, one launch (start us, length us, event | category | flops | bytes accessed | tf_op | source)
XLA Modules:
  0.0 96.5 jit_solution(14831490450817723411)
XLA Ops:
  0.6 0.0 copy-start
  0.7 5.6 %shard_map.131 = f32[16,2,1792]{2,1,0:T(2,128)} custom-call(s32[1]{0:T(128)} %bitcast.rep, f32[1,128,3584]{2,1,0:T(8,128)} %momentum.3, bf16[1,128,3584]{2,1,0:T(8,128)(2,1)} %grad.3, s32[96,2,1792]{2,1,0:T(2,128)} %chosen.3, bf16[2,128,128]{2,1,0:T(8,128)(2,1)} %constant.21.clone.left, bf16[2,256,256]{2,1,0:T(8,128)(2,1)} %constant.22.clone.right, ...), custom_call_target="tpu_custom_call" | custom-call | flops 1073741824 | bytes 3145728 | tf_op jit(solution)/shard_map/pallas_call | solution.py:321
  6.3 20.4 %all-to-all-start = ((f32[16,2,1792]{2,1,0:T(2,128)}), f32[16,2,1792]{2,1,0:T(2,128)S(1)}, u32[]{:S(2)}, u32[]{:S(2)}) async-start(f32[16,2,1792]{2,1,0:T(2,128)} %shard_map.131), calls=%async_computation | async-start | bytes 458752 | tf_op jit(solution)/shard_map/all_to_all | solution.py:335
  26.7 0.0 copy-done
  26.7 1.2 %copy.14 = s32[12,8,2,1792]{3,1,2,0:T(8,128)} copy(s32[12,8,2,1792]{3,2,1,0:T(2,128)S(1)} %bitcast.6) | data formatting | bytes 2752512
  27.9 7.3 %shard_map.132 = f32[1,128,3584]{2,1,0:T(8,128)} custom-call(s32[1]{0:T(128)} %bitcast.rep, f32[1,128,3584]{2,1,0:T(8,128)} %momentum.3, bf16[1,128,3584]{2,1,0:T(8,128)(2,1)} %grad.3, s32[96,2,1792]{2,1,0:T(2,128)} %chosen.3, bf16[2,128,128]{2,1,0:T(8,128)(2,1)} %constant.21.clone.left, bf16[2,256,256]{2,1,0:T(8,128)(2,1)} %constant.22.clone.right, ...), custom_call_target="tpu_custom_call" | custom-call | flops 2147483648 | bytes 5242880 | tf_op jit(solution)/shard_map/pallas_call | solution.py:336
  35.2 6.3 %shard_map.133 = (s32[896,128]{1,0:T(8,128)}, s32[7]{0:T(128)}) custom-call(s32[96,3584]{1,0:T(8,128)} %bitcast.7), custom_call_target="tpu_custom_call" | custom-call | flops 7516192768 | bytes 2097152 | tf_op jit(solution)/shard_map/pallas_call | solution.py:354
  41.6 0.0 all-to-all-done
  41.6 1.2 %broadcast_in_dim.8 = f32[6,16,3584]{2,1,0:T(8,128)} broadcast(f32[16,3584]{1,0:T(8,128)S(1)} %bitcast.10), dimensions={1,2} | broadcast | bytes 1605632 | tf_op jit(solution)/shard_map/broadcast_in_dim | solution.py:378
  42.8 4.4 %all-to-all-start.1 = ((f32[6,16,3584]{2,1,0:T(8,128)}), f32[6,16,3584]{2,1,0:T(8,128)S(1)}, u32[]{:S(2)}, u32[]{:S(2)}) async-start(f32[6,16,3584]{2,1,0:T(8,128)} %broadcast_in_dim.8), calls=%async_computation.1 | async-start | bytes 2752512 | tf_op jit(solution)/shard_map/all_to_all | solution.py:379
  47.2 16.0 %shard_map.134 = (s32[2688,128]{1,0:T(8,128)}, s32[21]{0:T(128)}) custom-call(s32[96,3584]{1,0:T(8,128)} %bitcast.8), custom_call_target="tpu_custom_call" | custom-call | flops 22548578304 | bytes 2097152 | tf_op jit(solution)/shard_map/pallas_call | solution.py:354
  63.3 4.0 %all-to-all-done.1 = f32[6,16,3584]{2,1,0:T(8,128)S(1)} async-done(((f32[6,16,3584]{2,1,0:T(8,128)}), f32[6,16,3584]{2,1,0:T(8,128)S(1)}, u32[]{:S(2)}, u32[]{:S(2)}) %all-to-all-start.1) | async-done | bytes 1376288 | tf_op jit(solution)/shard_map/all_to_all | solution.py:379
  67.3 0.0 copy-start.1
  67.3 1.1 %copy-done.1 = f32[6,16,3584]{2,1,0:T(8,128)} copy-done((f32[6,16,3584]{2,1,0:T(8,128)}, f32[6,16,3584]{2,1,0:T(8,128)S(1)}, u32[]{:S(2)}) %copy-start.1) | copy-done | bytes 1376280
  68.4 10.6 %shard_map.135 = (f32[3584,128]{1,0:T(8,128)}, f32[8,8,128]{2,1,0:T(8,128)}) custom-call(s32[7]{0:T(128)} %get-tuple-element.13.deep0, s32[21]{0:T(128)} %get-tuple-element.14.deep1, f32[96,3584]{1,0:T(8,128)} %bitcast.9, s32[896,128]{1,0:T(8,128)} %get-tuple-element.16.table0, s32[2688,128]{1,0:T(8,128)} %get-tuple-element.17.table1), custom_call_target="tpu_custom_call" | custom-call | flops 6442450944 | bytes 5242880 | tf_op jit(solution)/shard_map/pallas_call | solution.py:382
  79.0 8.3 %all-to-all-start.2 = ((f32[8,8,128]{2,1,0:T(8,128)}), f32[8,8,128]{2,1,0:T(8,128)S(1)}, u32[]{:S(2)}, u32[]{:S(2)}) async-start(f32[8,8,128]{2,1,0:T(8,128)} %get-tuple-element.19), calls=%async_computation.2 | async-start | bytes 65536 | tf_op jit(solution)/shard_map/all_to_all | solution.py:406
  87.2 5.4 %shard_map.136.decoded = f32[128,3584]{1,0:T(8,128)} custom-call(f32[3584,128]{1,0:T(8,128)} %get-tuple-element.18.summed, bf16[2,128,256]{2,1,0:T(8,128)(2,1)} %constant.27.clone.right, bf16[2,64,64]{2,1,0:T(8,128)(2,1)} %constant.28.clone.left), custom_call_target="tpu_custom_call" | custom-call | flops 1073741824 | bytes 4194304 | tf_op jit(solution)/shard_map/pallas_call | solution.py:408
  92.6 0.0 all-to-all-done.2.energy
  92.6 0.0 copy-start.2
  92.6 0.6 copy-done.2
  93.2 3.3 %shard_map.137 = f32[128,3584]{1,0:T(8,128)} custom-call(f32[128,3584]{1,0:T(8,128)} %weight.1, f32[128,3584]{1,0:T(8,128)} %shard_map.136.decoded, f32[8,8,128]{2,1,0:T(8,128)} %copy-done.2), custom_call_target="tpu_custom_call" | custom-call | flops 1048576 | bytes 6291456 | tf_op jit(solution)/shard_map/pallas_call | solution.py:423
  (1 shorter events, 0.0 us)
Async XLA Ops:
  0.6 26.1 %copy-start = (s32[96,2,1792]{2,1,0:T(2,128)S(1)}, s32[96,2,1792]{2,1,0:T(2,128)}, u32[]{:S(2)}) copy-start(s32[96,2,1792]{2,1,0:T(2,128)} %chosen.3) | copy-start | bytes 4128772
  6.3 35.3 %all-to-all-start = ((f32[16,2,1792]{2,1,0:T(2,128)}), f32[16,2,1792]{2,1,0:T(2,128)S(1)}, u32[]{:S(2)}, u32[]{:S(2)}) async-start(f32[16,2,1792]{2,1,0:T(2,128)} %shard_map.131), calls=%async_computation | async-start | bytes 458752 | tf_op jit(solution)/shard_map/all_to_all | solution.py:335
  42.8 24.4 %all-to-all-start.1 = ((f32[6,16,3584]{2,1,0:T(8,128)}), f32[6,16,3584]{2,1,0:T(8,128)S(1)}, u32[]{:S(2)}, u32[]{:S(2)}) async-start(f32[6,16,3584]{2,1,0:T(8,128)} %broadcast_in_dim.8), calls=%async_computation.1 | async-start | bytes 2752512 | tf_op jit(solution)/shard_map/all_to_all | solution.py:379
  67.3 1.1 %copy-start.1 = (f32[6,16,3584]{2,1,0:T(8,128)}, f32[6,16,3584]{2,1,0:T(8,128)S(1)}, u32[]{:S(2)}) copy-start(f32[6,16,3584]{2,1,0:T(8,128)S(1)} %all-to-all-done.1) | copy-start | bytes 4128772
  79.0 13.7 %all-to-all-start.2 = ((f32[8,8,128]{2,1,0:T(8,128)}), f32[8,8,128]{2,1,0:T(8,128)S(1)}, u32[]{:S(2)}, u32[]{:S(2)}) async-start(f32[8,8,128]{2,1,0:T(8,128)} %get-tuple-element.19), calls=%async_computation.2 | async-start | bytes 65536 | tf_op jit(solution)/shard_map/all_to_all | solution.py:406
  92.6 0.6 copy-start.2
